TPU v7x, 1024 devices: a whole 8x8x8 slice. The times are simulated.
1024 devices in a mesh: row: 32 (over z, y_hi, core), col: 32 (over x, y_lo).
Axes of the slice: x: 8, y: 8 (y_hi: 2, y_lo: 4; y = y_hi * 4 + y_lo), z: 8, core: 2. Of those that a mesh axis runs over, the one named last changes fastest.
Arguments:
- matrix_blocks: bfloat16 [32, 128, 4096], P('row', 'col'), may hold values from -6 to 6
- block_codes: int32 [32, 128], P('row', 'col'), may hold values from 0 to 16383, as said below
- block_perm: int32 [128], replicated, may hold values from 0 to 127, as said below
- grid_blocks: bfloat16 [32, 2048, 4096], P('row', 'col'), may hold values from -2.4 to 2.4, as said below
- grid_tasks: int32 [32, 2048], P('row', 'col'), may hold values from -1 to 16383, as said below
Outputs:
- square: bfloat16 [32, 128, 4096], P('row', 'col')
- sign_next: bfloat16 [32, 128, 4096], P('row', 'col')
Inputs may be any that keep to these rules, and one draw needn't show every extreme that they name: `block_perm`: A permutation of 0 to 127. `block_codes`: index (r, c) stores 4 different positions, each with block row in [r * 4, (r + 1) * 4) and block column in [c * 4, (c + 1) * 4). `grid_tasks`: index (r, c) holds 32 groups of 2 slots; a live item in group j names a position stored by index (r, j); in every index of row one owner receives 2 live items from every sender of its row. `grid_blocks`: empty slots hold zeros.
All inputs are finite; a program needn't handle non-finite values.
Results may differ from a plain program's by a relative error of at most 0.0058.
Values may be sent and summed in bfloat16 or wider, within the bound.
No kernel may reach another device: no remote copies, remote signals or barrier semaphores. Data moves between devices by JAX's collectives and lax.ppermute only.
A program may use at most 64 MiB of HBM per device.

v0:
```python
import math

import jax
import jax.numpy as jnp
from jax import lax
from jax.sharding import PartitionSpec as P

BS = 64


def lookup(indices, table):
    positions = jnp.arange(table.shape[0], dtype=jnp.int32)
    return jnp.sum(jnp.where(indices[:, None] == positions[None, :], table[None, :], 0), axis=1)


def tile_terms(
    left_panel, left_codes_all, right_blocks, right_codes, own_codes, block_count, tile_cols
):
    right_row = right_codes // block_count
    right_col = right_codes % block_count
    tile_index = right_row // tile_cols
    left_blocks = jnp.take(left_panel, tile_index, axis=0)
    left_codes = jnp.take(left_codes_all, tile_index, axis=0)
    left_row = left_codes // block_count
    left_col = left_codes % block_count
    own_row = own_codes // block_count
    own_col = own_codes % block_count
    selector = (
        (left_row[None] == own_row[:, None, None])
        & (left_col[None] == right_row[None, :, None])
        & (right_col[None, :, None] == own_col[:, None, None])
    )
    chosen = jnp.einsum(
        "cba,baik->cbik",
        selector.astype(jnp.bfloat16),
        left_blocks,
        preferred_element_type=jnp.bfloat16,
    )
    return jnp.einsum("cbik,bkj->cij", chosen, right_blocks, preferred_element_type=jnp.float32)


def local(matrix_blocks, block_codes, block_perm, grid_blocks, grid_tasks):
    col_count = lax.axis_size("col")
    row_count = lax.axis_size("row")
    block_count = block_perm.shape[0]
    slot_count = block_codes.shape[1]
    tile_cols = block_count // col_count
    received, arrived = (
        lax.all_to_all(grid_blocks, "col", split_axis=1, concat_axis=1, tiled=True),
        lax.all_to_all(grid_tasks, "col", split_axis=1, concat_axis=1, tiled=True),
    )
    task_list = arrived[0]
    is_live = task_list >= 0
    task_safe = jnp.where(is_live, task_list, 0)
    position = lookup(task_safe // block_count, block_perm) * block_count + lookup(
        task_safe % block_count, block_perm
    )
    own_codes = block_codes[0]
    matches = ((position[:, None] == own_codes[None, :]) & is_live[:, None]).astype(jnp.bfloat16)
    grid_sum = jnp.einsum("ms,mf->sf", matches, received[0], preferred_element_type=jnp.float32)
    matrix = (matrix_blocks[0].astype(jnp.float32) + grid_sum).astype(jnp.bfloat16)
    stacked = matrix[None]
    panel_data, panel_codes = (
        lax.all_gather(stacked, "col", axis=1, tiled=True),
        lax.all_gather(block_codes, "col", axis=1, tiled=True),
    )
    panel_tiles = panel_data[0].reshape(col_count, slot_count, BS, BS)
    panel_tile_codes = panel_codes[0].reshape(col_count, slot_count)

    def accumulate(block_piece):
        piece_data, piece_codes = block_piece
        return tile_terms(
            panel_tiles,
            panel_tile_codes,
            piece_data.reshape(-1, BS, BS),
            piece_codes.reshape(-1),
            own_codes,
            block_count,
            tile_cols,
        )

    scale_factor = 1.5 / math.sqrt(BS * slot_count * col_count / (block_count // row_count))
    product_one = accumulate(
        (
            lax.all_gather(stacked, "row", axis=0, tiled=True),
            lax.all_gather(block_codes, "row", axis=0, tiled=True),
        )
    )
    square = (scale_factor * product_one).reshape(slot_count, BS * BS).astype(jnp.bfloat16)
    square_stacked = square[None]
    second = accumulate(
        (
            lax.all_gather(square_stacked, "row", axis=0, tiled=True),
            lax.all_gather(block_codes, "row", axis=0, tiled=True),
        )
    )
    sign_next = (
        1.5 * matrix.astype(jnp.float32) - 0.5 * scale_factor * second.reshape(slot_count, BS * BS)
    ).astype(jnp.bfloat16)
    return (square_stacked, sign_next[None])


def solution(mesh):
    in_specs = (P("row", "col", None), P("row", "col"), P(), P("row", "col", None), P("row", "col"))
    out_specs = (P("row", "col", None), P("row", "col", None))
    return jax.shard_map(local, mesh=mesh, in_specs=in_specs, out_specs=out_specs, check_vma=False)
```

profile of v0, /device:TPU:1, one launch (start us, length us, event | category | flops | bytes accessed | tf_op | source)
XLA Modules:
  0.0 434.7 jit_solution(2914158998377224226)
XLA Ops:
  7.2 0.6 broadcast.291
  7.8 1.4 reduce.9
  9.1 0.7 all_to_all.9
  9.8 11.1 %all-to-all-start = ((s32[1,32,2]{2,0,1:T(1,128)}), s32[1,32,2]{2,0,1:T(1,128)S(1)}, u32[]{:S(2)}, u32[]{:S(2)}) async-start(s32[1,32,2]{2,0,1:T(1,128)} %bitcast.2), calls=%async_computation | async-start | bytes 32768 | tf_op jit(solution)/shard_map/all_to_all | solution.py:50
  20.9 2.2 copy.58
  23.1 0.5 broadcast.296
  23.6 3.8 reduce.12
  27.4 1.1 reshape.306
  28.6 1.2 all-to-all-done
  29.8 8.3 %all-to-all-start.1 = ((bf16[32,2,4096]{2,1,0:T(2,128)(2,1)}), bf16[32,2,4096]{2,1,0:T(2,128)(2,1)S(1)}, u32[]{:S(2)}, u32[]{:S(2)}) async-start(bf16[32,2,4096]{2,1,0:T(2,128)(2,1)} %reshape.306), calls=%async_computation.1 | async-start | bytes 1048576 | tf_op jit(solution)/shard_map/all_to_all | solution.py:49
  38.1 0.0 all-gather.11.cloned.1.call-start
  38.1 0.7 reduce.10
  38.9 0.1 squeeze.8
  39.0 0.8 select_reduce_fusion.1
  39.9 11.5 %all-to-all-done.1 = bf16[32,2,4096]{2,1,0:T(2,128)(2,1)S(1)} async-done(((bf16[32,2,4096]{2,1,0:T(2,128)(2,1)}), bf16[32,2,4096]{2,1,0:T(2,128)(2,1)S(1)}, u32[]{:S(2)}, u32[]{:S(2)}) %all-to-all-start.1) | async-done | bytes 524320 | tf_op jit(solution)/shard_map/all_to_all | solution.py:49
  51.4 0.5 reshape.307
  51.9 2.1 fusion.9
  54.0 0.0 all-gather.11.cloned.1.call-update
  54.0 0.0 all-gather.13.cloned.1.call-start
  54.1 70.3 %all-gather.3 = s32[32,1,4]{2,1,0:T(1,128)S(1)} all-gather(s32[1,1,4]{2,1,0:T(1,128)} %bitcast.51), channel_id=1, replica_groups=mesh['row'=32,'col'=32] {'row'}, dimensions={0}, use_global_device_ids=true | all-gather | bytes 528 | tf_op jit(solution)/shard_map/all_gather | solution.py:86
  124.4 0.7 reduce.11
  125.1 0.1 reshape.231
  125.2 1.3 dynamic-slice
  127.2 0.7 and_select_fusion
  127.9 11.3 %all-reduce = s32[128]{0:T(128)S(1)} all-reduce(s32[128]{0:T(128)S(1)} %get-tuple-element.12), channel_id=1, replica_groups=mesh['row'=32,'col'=32] {'col'}, use_global_device_ids=true, to_apply=%add | all-reduce | flops 128 | bytes 1024
  139.2 0.1 reshape_squeeze.7
  139.4 0.6 gather_fusion.1
  140.0 0.1 broadcast_compare_fusion
  140.1 0.1 fusion.35
  140.2 0.1 add_select_fusion.1
  140.4 0.0 all-gather.13.cloned.1.call-update
  140.4 0.2 all-gather.9.cloned.1.call-start
  140.6 57.5 %all-gather.11.cloned.1.call-done = bf16[32,4,4096]{2,1,0:T(4,128)(2,1)} async-done(((bf16[1,4,4096]{2,1,0:T(4,128)(2,1)}), bf16[32,4,4096]{2,1,0:T(4,128)(2,1)}) %all-gather.11.cloned.1.call-update) | async-done | bytes 1048592 | tf_op jit(solution)/shard_map/all_gather | solution.py:64
  198.1 3.3 reshape_squeeze.6
  201.4 6.6 %gather_fusion = bf16[128,4,64,64]{3,2,1,0:T(8,128)(2,1)} fusion(bf16[32,4,64,64]{3,2,1,0:T(8,128)(2,1)S(1)} %reshape_squeeze.6, s32[1024]{0:T(1024)S(1)} %pad_clamp_fusion), kind=kCustom, calls=%fused_computation.clone | custom fusion | bytes 8389120 | tf_op jit(solution)/shard_map/jit(_take)/gather | solution.py:22
  208.0 7.4 %broadcast_select_fusion = bf16[128,4,64,64]{3,2,1,0:T(8,128)(2,1)} fusion(bf16[128,4,64,64]{3,2,1,0:T(8,128)(2,1)} %gather_fusion, pred[128]{0:T(512)(128)(4,1)S(1)} %get-tuple-element.6), kind=kLoop, calls=%fused_computation.4 | loop fusion | flops 2097152 | bytes 8388736 | tf_op jit(solution)/shard_map/jit(_take)/select_n | solution.py:22
  215.4 12.4 %fusion.6 = bf16[4,128,64,64]{3,0,2,1:T(4,128)(2,1)} fusion(bf16[128,4,64,64]{3,2,1,0:T(8,128)(2,1)} %broadcast_select_fusion, s32[128,4]{1,0:T(8,128)S(1)} %add_select_fusion.1, s32[4]{0:T(128)S(1)} %get-tuple-element.13, pred[4,128]{0,1:T(8,128)(4,1)S(1)} %broadcast_compare_fusion, pred[128,4]{1,0:T(8,128)(4,1)S(1)} %fusion.35), kind=kOutput, calls=%fused_computation.9 | convolution fusion | flops 16783360 | bytes 8391696 | tf_op jit(solution)/shard_map/cba,baik->cbik/dot_general | solution.py:33
  227.7 93.2 %all-gather.13.cloned.1.call-done = bf16[32,4,4096]{2,1,0:T(4,128)(2,1)} async-done(((bf16[1,4,4096]{2,1,0:T(4,128)(2,1)}), bf16[32,4,4096]{2,1,0:T(4,128)(2,1)}) %all-gather.13.cloned.1.call-update) | async-done | bytes 1048592 | tf_op jit(solution)/shard_map/all_gather | solution.py:85
  321.0 3.3 reshape.277
  324.3 5.4 %fusion.22 = bf16[4,64,64]{2,1,0:T(8,128)(2,1)S(1)} fusion(bf16[128,64,64,1]{2,1,0,3:T(8,128)(2,1)S(1)} %reshape.277, bf16[4,128,64,64]{3,0,2,1:T(4,128)(2,1)} %fusion.6), kind=kOutput, calls=%fused_computation.16 | convolution fusion | flops 268468224 | bytes 5275648 | tf_op jit(solution)/shard_map/cbik,bkj->cij/dot_general | solution.py:39
  329.7 0.7 convert_element_type.35
  330.4 0.0 all-gather.9.cloned.1.call-update
  330.4 0.0 copy-start
  330.4 88.3 %all-gather.9.cloned.1.call-done = bf16[32,4,4096]{2,1,0:T(4,128)(2,1)} async-done(((bf16[1,4,4096]{2,1,0:T(4,128)(2,1)}), bf16[32,4,4096]{2,1,0:T(4,128)(2,1)}) %all-gather.9.cloned.1.call-update) | async-done | bytes 1048592 | tf_op jit(solution)/shard_map/all_gather | solution.py:93
  418.7 3.3 reshape.279
  422.0 5.4 %fusion.16 = f32[4,64,64]{2,1,0:T(8,128)S(1)} fusion(bf16[128,64,64,1]{2,1,0,3:T(8,128)(2,1)S(1)} %reshape.279, bf16[4,128,64,64]{3,0,2,1:T(4,128)(2,1)} %fusion.6), kind=kOutput, calls=%fused_computation.14 | convolution fusion | flops 268451840 | bytes 5308416 | tf_op jit(solution)/shard_map/cbik,bkj->cij/dot_general | solution.py:39
  427.4 0.1 mul.36
  427.5 0.0 copy-done
  427.5 0.6 fusion.38
  (8 shorter events, 0.1 us)
Async XLA Ops:
  9.8 20.0 %all-to-all-start = ((s32[1,32,2]{2,0,1:T(1,128)}), s32[1,32,2]{2,0,1:T(1,128)S(1)}, u32[]{:S(2)}, u32[]{:S(2)}) async-start(s32[1,32,2]{2,0,1:T(1,128)} %bitcast.2), calls=%async_computation | async-start | bytes 32768 | tf_op jit(solution)/shard_map/all_to_all | solution.py:50
  29.8 21.6 %all-to-all-start.1 = ((bf16[32,2,4096]{2,1,0:T(2,128)(2,1)}), bf16[32,2,4096]{2,1,0:T(2,128)(2,1)S(1)}, u32[]{:S(2)}, u32[]{:S(2)}) async-start(bf16[32,2,4096]{2,1,0:T(2,128)(2,1)} %reshape.306), calls=%async_computation.1 | async-start | bytes 1048576 | tf_op jit(solution)/shard_map/all_to_all | solution.py:49
  38.1 160.0 %all-gather.11.cloned.1.call-start = ((), (), s32[]{:S(2)}) async-start(), calls=%async_computation.3 | async-start | bytes 1081344 | tf_op jit(solution)/shard_map/all_gather | solution.py:64
  54.0 267.0 %all-gather.13.cloned.1.call-start = ((), (), s32[]{:S(2)}) async-start(), calls=%async_computation.4 | async-start | bytes 1081344 | tf_op jit(solution)/shard_map/all_gather | solution.py:85
  140.4 278.3 %all-gather.9.cloned.1.call-start = ((), (), s32[]{:S(2)}) async-start(), calls=%async_computation.2 | async-start | bytes 1081344 | tf_op jit(solution)/shard_map/all_gather | solution.py:93
  330.4 97.1 %copy-start = (bf16[4,4096]{1,0:T(4,128)(2,1)S(1)}, bf16[4,4096]{1,0:T(4,128)(2,1)}, u32[]{:S(2)}) copy-start(bf16[4,4096]{1,0:T(4,128)(2,1)} %fusion.9) | copy-start | bytes 98308
Sparse Core Ops, SparseCore 0:
  54.1 143.9 all-gather.10
  203.2 117.7 all-gather.12
  330.6 88.1 all-gather.8
where the time goes:
time: 436 us; the launch traced here: 435 us
  waiting for transfers between devices  252 us (58%)
  blocking collectives  81.6 us (19%)
  local copies, waits for them, and re-layouts  25.2 us (6%)
  matrix products  25.2 us (6%)
  starting transfers between devices  19.7 us (5%)
  other arithmetic  16.6 us (4%)
  between operations  14.6 us (3%)
    all_gather x1, waiting for transfers between devices, local(): lax.all_gather(stacked, 'row', axis=0, tiled=True)  93.2 us
    all_gather x1, waiting for transfers between devices, local(): lax.all_gather(square_stacked, 'row', axis=0, tiled=True)  88.3 us
    all_gather x1, blocking collectives, local(): lax.all_gather(block_codes, 'row', axis=0, tiled=True)  70.3 us
    all_gather x1, waiting for transfers between devices, local(): lax.all_gather(stacked, 'col', axis=1, tiled=True)  57.5 us
    dot_general x1, matrix products, tile_terms(): jnp.einsum('cba,baik->cbik', selector.astype(jnp.bfloat16), left_blocks,...  12.4 us
    all_to_all x1, waiting for transfers between devices, local(): lax.all_to_all(grid_blocks, 'col', split_axis=1, concat_axis=1, tiled=True)  11.5 us
    unnamed x1, blocking collectives  11.3 us
    all_to_all x1, starting transfers between devices, local(): lax.all_to_all(grid_tasks, 'col', split_axis=1, concat_axis=1, tiled=True)  11.1 us
  transfers between devices with their start and end apart: 5, of which 5 were waited for; matrix products, arithmetic and copies ran while one was open for 10% of the time, Pallas kernels for 0%

commit v1 on v0

v1 whole, which is shorter than its diff:
```python
import math

import jax
import jax.numpy as jnp
from jax import lax
from jax.experimental import pallas as pl
from jax.experimental.pallas import tpu as pltpu
from jax.sharding import PartitionSpec as P

BS = 64
SLOTS = 4
SIDE = 4
TILE = BS * SIDE
VMEM = pl.BlockSpec(memory_space=pltpu.VMEM)
SMEM = pl.BlockSpec(memory_space=pltpu.SMEM)


def lookup(indices, table):
    positions = jnp.arange(table.shape[0], dtype=jnp.int32)
    return jnp.sum(jnp.where(indices[:, None] == positions[None, :], table[None, :], 0), axis=1)


def pack(blocks):
    return blocks.reshape(2, 2, BS, BS).transpose(0, 2, 1, 3).reshape(2, BS, 2 * BS)


def unpack(pairs):
    return pairs.reshape(2, BS, 2, BS).transpose(0, 2, 1, 3).reshape(SLOTS, BS * BS)


def swap_halves(x):
    return jnp.concatenate([x[:, BS:], x[:, :BS]], axis=1)


def place(dense, row, column, pair, slot, where_, masks):
    half = where_ % 2
    moved = jnp.where(half == slot % 2, pair, swap_halves(pair))
    kept = moved * jnp.where(half == 0, masks[0], masks[1])
    rows = pl.ds(pl.multiple_of(row + (where_ // SIDE) * BS, BS), BS)
    columns = pl.ds(pl.multiple_of(column + ((where_ % SIDE) // 2) * 2 * BS, 2 * BS), 2 * BS)
    dense[rows, columns] = dense[rows, columns] + kept


def lane_masks():
    lane = lax.broadcasted_iota(jnp.int32, (BS, 2 * BS), 1)
    low = jnp.where(lane < BS, 1.0, 0.0).astype(jnp.bfloat16)
    return low, (1.0 - low.astype(jnp.float32)).astype(jnp.bfloat16)


def fill_left(dense, panel, codes):
    masks = lane_masks()
    dense[...] = jnp.zeros_like(dense)

    def body(t, carry):
        for slot in range(SLOTS):
            place(dense, 0, t * TILE, panel[t, slot // 2], slot, codes[t * SLOTS + slot], masks)
        return carry

    lax.fori_loop(0, panel.shape[0], body, 0)


def fill_right(dense, panels, codes, core):
    masks = lane_masks()
    dense[...] = jnp.zeros_like(dense)
    for which, panel in enumerate(panels):

        def body(a, carry, which=which, panel=panel):
            t = 2 * a + (core if which == 0 else 1 - core)
            for slot in range(SLOTS):
                pair = panel[a, pl.ds((slot // 2) * BS, BS), :]
                place(dense, t * TILE, 0, pair, slot, codes[t * SLOTS + slot], masks)
            return carry

        lax.fori_loop(0, panel.shape[0], body, 0)


def own_pairs(total, own):
    lane = lax.broadcasted_iota(jnp.int32, (BS, 2 * BS), 1)
    pairs = []
    for pair in range(2):
        parts = []
        for slot in (2 * pair, 2 * pair + 1):
            where_ = own[slot]
            rows = pl.ds(pl.multiple_of((where_ // SIDE) * BS, BS), BS)
            columns = pl.ds(pl.multiple_of(((where_ % SIDE) // 2) * 2 * BS, 2 * BS), 2 * BS)
            block = total[rows, columns]
            parts.append(jnp.where(where_ % 2 == slot % 2, block, pltpu.roll(block, BS, 1)))
        pairs.append(jnp.where(lane < BS, parts[0], parts[1]))
    return pairs


def first_kernel(
    scale, codes_left, codes_right, own, core, left, mine, other, square, dense_left, dense_right, total
):
    fill_right(dense_right, (mine, other), codes_right, core[0])
    fill_left(dense_left, left, codes_left)
    total[...] = jnp.dot(dense_left[...], dense_right[...], preferred_element_type=jnp.float32)
    for pair, value in enumerate(own_pairs(total, own)):
        square[pair] = (scale * value).astype(square.dtype)


def second_kernel(
    scale, codes_right, own, core, dense_left, mine, other, matrix, sign_next, dense_right, total
):
    fill_right(dense_right, (mine, other), codes_right, core[0])
    total[...] = jnp.dot(dense_left[...], dense_right[...], preferred_element_type=jnp.float32)
    for pair, value in enumerate(own_pairs(total, own)):
        before = matrix[pair].astype(jnp.float32)
        sign_next[pair] = (1.5 * before - 0.5 * scale * value).astype(sign_next.dtype)


def local(matrix_blocks, block_codes, block_perm, grid_blocks, grid_tasks):
    col_count = lax.axis_size("col")
    row_count = lax.axis_size("row")
    block_count = block_perm.shape[0]
    tile_rows = block_count // row_count
    tile_cols = block_count // col_count
    bf16 = jnp.bfloat16
    barrier = lax.optimization_barrier
    core = lax.axis_index("row") % 2
    own_codes = block_codes[0]
    own_place = (own_codes // block_count) % tile_rows * SIDE + own_codes % tile_cols

    tasks = grid_tasks[0]
    safe = jnp.maximum(tasks, 0)
    place_row = lookup(safe // block_count, block_perm) % tile_rows
    place_col = lookup(safe % block_count, block_perm) % tile_cols
    item_place = jnp.where(tasks >= 0, place_row * SIDE + place_col, -1)
    cap = tasks.shape[0] // col_count
    tail = jnp.concatenate(
        [
            item_place[:, None].astype(bf16),
            jnp.broadcast_to(own_place.astype(bf16)[None], (tasks.shape[0], SLOTS)),
            jnp.zeros((tasks.shape[0], 128 - 1 - SLOTS), bf16),
        ],
        axis=1,
    )
    payload = jnp.concatenate([grid_blocks[0], tail], axis=1).reshape(col_count, cap, -1)
    received = lax.all_to_all(payload, "col", 0, 0, tiled=True)
    codes_left = received[:, 0, BS * BS + 1 : BS * BS + 1 + SLOTS].astype(jnp.int32).reshape(-1)
    arrived_place = received[:, :, BS * BS].astype(jnp.int32).reshape(-1)
    items = received[:, :, : BS * BS].reshape(-1, BS * BS)
    matches = (own_place[:, None] == arrived_place[None, :]).astype(bf16)
    grid_sum = jnp.dot(matches, items, preferred_element_type=jnp.float32)
    matrix = (matrix_blocks[0].astype(jnp.float32) + grid_sum).astype(bf16)
    pairs = barrier(pack(matrix))

    runs = [[x * 4 + y for y in range(4)] for x in range(col_count // 4)]
    lines = [[x * 4 + y for x in range(col_count // 4)] for y in range(4)]
    near = lax.all_to_all(
        jnp.broadcast_to(pairs[None], (4,) + pairs.shape),
        "col", 0, 0, axis_index_groups=runs, tiled=True,
    )
    left = lax.all_to_all(
        jnp.broadcast_to(near[None], (col_count // 4,) + near.shape),
        "col", 0, 0, axis_index_groups=lines, tiled=True,
    ).reshape((col_count,) + pairs.shape)

    cores = [[2 * chip + one for chip in range(row_count // 2)] for one in range(2)]
    swap = [(i, i ^ 1) for i in range(row_count)]

    def column_panel(rows):
        chips = row_count // 2
        mine = lax.all_to_all(
            jnp.broadcast_to(rows[None], (chips,) + rows.shape),
            "row", 0, 0, axis_index_groups=cores, tiled=True,
        )
        return mine, lax.ppermute(mine, "row", swap)

    code_rows = jnp.zeros((16, 128), bf16).at[0, :SLOTS].set(own_place.astype(bf16))
    mine, other = column_panel(jnp.concatenate([pairs.reshape(2 * BS, 2 * BS), code_rows], axis=0))
    codes_mine = mine[:, 2 * BS, :SLOTS].astype(jnp.int32)
    codes_other = other[:, 2 * BS, :SLOTS].astype(jnp.int32)
    is_even = core == 0
    codes_right = jnp.stack(
        [jnp.where(is_even, codes_mine, codes_other), jnp.where(is_even, codes_other, codes_mine)],
        axis=1,
    ).reshape(-1)

    scale = 1.5 / math.sqrt(BS * SLOTS * col_count / (block_count // row_count))
    depth = col_count * TILE
    core_word = core.astype(jnp.int32).reshape(1)
    params = pltpu.CompilerParams(vmem_limit_bytes=48 * 1024 * 1024)
    square, dense_left = pl.pallas_call(
        lambda *refs: first_kernel(scale, *refs),
        out_shape=(
            jax.ShapeDtypeStruct(pairs.shape, bf16),
            jax.ShapeDtypeStruct((TILE, depth), bf16),
        ),
        in_specs=[SMEM] * 4 + [VMEM] * 3,
        out_specs=(VMEM, VMEM),
        scratch_shapes=[pltpu.VMEM((depth, TILE), bf16), pltpu.VMEM((TILE, TILE), jnp.float32)],
        compiler_params=params,
    )(codes_left, codes_right, own_place, core_word, left, mine, other)

    mine, other = column_panel(square.reshape(2 * BS, 2 * BS))
    sign_next = pl.pallas_call(
        lambda *refs: second_kernel(scale, *refs),
        out_shape=jax.ShapeDtypeStruct(pairs.shape, bf16),
        in_specs=[SMEM] * 3 + [VMEM] * 4,
        out_specs=VMEM,
        scratch_shapes=[pltpu.VMEM((depth, TILE), bf16), pltpu.VMEM((TILE, TILE), jnp.float32)],
        compiler_params=params,
    )(codes_right, own_place, core_word, dense_left, mine, other, pairs)
    return (unpack(square)[None], unpack(sign_next)[None])


def solution(mesh):
    in_specs = (P("row", "col", None), P("row", "col"), P(), P("row", "col", None), P("row", "col"))
    out_specs = (P("row", "col", None), P("row", "col", None))
    return jax.shard_map(local, mesh=mesh, in_specs=in_specs, out_specs=out_specs, check_vma=False)
```

time: 436 us -> 171 us (0.39)
  the two profiles are of different devices: /device:TPU:1 before, /device:TPU:17 now
where the time goes in v1:
time: 171 us; the launch traced here: 170 us
  blocking collectives  70.1 us (41%)
  waiting for transfers between devices  40.9 us (24%)
  starting transfers between devices  25.8 us (15%)
  Pallas kernels  15.8 us (9%)
  local copies, waits for them, and re-layouts  12.1 us (7%)
  other arithmetic  4.38 us (3%)
    all_to_all x2, blocking collectives, column_panel(): lax.all_to_all(jnp.broadcast_to(rows[None], (chips,) + rows.shape), 'row'...  70.1 us
    all_to_all x1, waiting for transfers between devices, local(): lax.all_to_all(jnp.broadcast_to(near[None], (col_count // 4,) + near.shap...  23.3 us
    all_to_all x1, waiting for transfers between devices, local(): received = lax.all_to_all(payload, 'col', 0, 0, tiled=True)  11.3 us
    pallas_call x1, Pallas kernels, local(): pl.pallas_call(lambda *refs: first_kernel(scale, *refs), out_shape=(jax.S...  10.6 us
    all_to_all x1, starting transfers between devices, local(): received = lax.all_to_all(payload, 'col', 0, 0, tiled=True)  10.1 us
    ppermute x2, starting transfers between devices, column_panel(): return (mine, lax.ppermute(mine, 'row', swap))  7.04 us
    pallas_call x1, Pallas kernels, local(): pl.pallas_call(lambda *refs: second_kernel(scale, *refs), out_shape=jax.S...  5.24 us
    all_to_all x1, starting transfers between devices, local(): lax.all_to_all(jnp.broadcast_to(pairs[None], (4,) + pairs.shape), 'col',...  4.95 us
  transfers between devices with their start and end apart: 5, of which 5 were waited for; matrix products, arithmetic and copies ran while one was open for 1% of the time, Pallas kernels for 0%

profile of v1, /device:TPU:17, one launch (start us, length us, event | category | flops | bytes accessed | tf_op | source)
XLA Modules:
  0.0 170.3 jit_solution(10845439578374955291)
XLA Ops:
  0.6 0.0 copy-start.2
  0.6 0.0 copy-start.1
  0.7 0.7 compare_reduce_fusion
  1.3 0.7 and_select_fusion.7
  2.0 0.7 fusion.20
  2.7 0.1 ge.15
  2.8 0.1 copy.33
  2.9 0.9 select_reduce_fusion.1
  3.7 0.1 reduce_sum.23
  3.9 0.1 copy.27
  3.9 0.1 reduce_sum.25
  4.0 0.1 copy.30
  4.2 0.1 copy.34
  4.3 1.4 concatenate.11
  5.7 2.8 %concatenate.12 = bf16[32,2,4224]{2,1,0:T(2,128)(2,1)} concatenate(bf16[32,2,4096]{2,1,0:T(2,128)(2,1)S(1)} %concatenate.11, bf16[32,2,1]{2,1,0:T(2,128)(2,1)S(1)} %copy.34, bf16[32,2,4]{2,1,0:T(2,128)(2,1)S(1)} %broadcast_in_dim.37, bf16[32,2,123]{2,1,0:T(2,128)(2,1)S(1)} %broadcast_in_dim.38), dimensions={2} | concatenate | bytes 1081344 | tf_op jit(solution)/shard_map/concatenate | solution.py:138
  8.5 10.1 %all-to-all-start = ((bf16[32,2,4224]{2,1,0:T(2,128)(2,1)}), bf16[32,2,4224]{2,1,0:T(2,128)(2,1)S(1)}, u32[]{:S(2)}, u32[]{:S(2)}) async-start(bf16[32,2,4224]{2,1,0:T(2,128)(2,1)} %concatenate.12), calls=%async_computation | async-start | bytes 1081344 | tf_op jit(solution)/shard_map/all_to_all | solution.py:139
  18.5 0.7 fusion.13.refs_2_.refs_1_
  19.2 11.3 %all-to-all-done = bf16[32,2,4224]{2,1,0:T(2,128)(2,1)S(1)} async-done(((bf16[32,2,4224]{2,1,0:T(2,128)(2,1)}), bf16[32,2,4224]{2,1,0:T(2,128)(2,1)S(1)}, u32[]{:S(2)}, u32[]{:S(2)}) %all-to-all-start) | async-done | bytes 540704 | tf_op jit(solution)/shard_map/all_to_all | solution.py:139
  30.5 0.6 convert_reduce_fusion
  31.1 0.1 reshape.322
  31.2 0.5 slice.38
  31.8 0.2 reshape.311
  32.0 0.0 copy-done.1
  32.0 0.2 fusion
  32.3 0.1 reshape.312
  32.4 0.1 copy.39
  32.5 0.1 reshape.313.refs_6_
  32.6 0.7 broadcast_in_dim.69
  33.2 4.9 %all-to-all-start.2 = ((bf16[4,2,64,128]{3,2,1,0:T(8,128)(2,1)}), bf16[4,2,64,128]{3,2,1,0:T(8,128)(2,1)S(1)}, u32[]{:S(2)}, u32[]{:S(2)}) async-start(bf16[4,2,64,128]{3,2,1,0:T(8,128)(2,1)} %broadcast_in_dim.69), calls=%async_computation.2 | async-start | bytes 262144 | tf_op jit(solution)/shard_map/all_to_all | solution.py:150
  38.2 0.0 copy-done.2
  38.2 4.3 %all-to-all-done.2 = bf16[4,2,64,128]{3,2,1,0:T(8,128)(2,1)S(1)} async-done(((bf16[4,2,64,128]{3,2,1,0:T(8,128)(2,1)}), bf16[4,2,64,128]{3,2,1,0:T(8,128)(2,1)S(1)}, u32[]{:S(2)}, u32[]{:S(2)}) %all-to-all-start.2) | async-done | bytes 131104 | tf_op jit(solution)/shard_map/all_to_all | solution.py:150
  42.5 0.1 broadcast_in_dim.68
  42.6 45.3 %all_to_all.25.refs_5_ = bf16[16,144,128]{2,1,0:T(8,128)(2,1)S(1)} all-to-all(bf16[16,144,128]{2,1,0:T(8,128)(2,1)S(1)} %broadcast_in_dim.68), channel_id=1, replica_groups={{0,64,128,192,256,320,384,448,512,576,640,704,768,832,896,960},{32,96,1..., dimensions={0} | all-to-all | bytes 1179648 | tf_op jit(solution)/shard_map/all_to_all | solution.py:164
  87.9 1.2 broadcast_in_dim.70
  89.2 3.8 %all-to-all-start.3 = ((bf16[8,4,2,64,128]{4,3,2,1,0:T(8,128)(2,1)}), bf16[8,4,2,64,128]{4,3,2,1,0:T(8,128)(2,1)S(1)}, u32[]{:S(2)}, u32[]{:S(2)}) async-start(bf16[8,4,2,64,128]{4,3,2,1,0:T(8,128)(2,1)} %broadcast_in_dim.70), calls=%async_computation.3 | async-start | bytes 2097152 | tf_op jit(solution)/shard_map/all_to_all | solution.py:154
  92.9 4.1 %collective-permute-start = (bf16[16,144,128]{2,1,0:T(8,128)(2,1)S(1)}, bf16[16,144,128]{2,1,0:T(8,128)(2,1)S(1)}, u32[]{:S(2)}, u32[]{:S(2)}) collective-permute-start(bf16[16,144,128]{2,1,0:T(8,128)(2,1)S(1)} %all_to_all.25.refs_5_), channel_id=1, source_target_pairs={{0,32},{32,0},{64,96},{96,64},{128,160},{160,128},{192,224},{224,1... | collective-permute-start | bytes 1769480 | tf_op jit(solution)/shard_map/ppermute | solution.py:168
  97.1 0.1 fusion.3
  97.2 0.1 reshape.320.refs_0_
  97.3 1.4 collective-permute-done.refs_6_
  98.7 0.1 reshape.315.refs_1_.refs_0_
  98.8 23.3 %all-to-all-done.3 = bf16[8,4,2,64,128]{4,3,2,1,0:T(8,128)(2,1)S(1)} async-done(((bf16[8,4,2,64,128]{4,3,2,1,0:T(8,128)(2,1)}), bf16[8,4,2,64,128]{4,3,2,1,0:T(8,128)(2,1)S(1)}, u32[]{:S(2)}, u32[]{:S(2)}) %all-to-all-start.3) | async-done | bytes 1048608 | tf_op jit(solution)/shard_map/all_to_all | solution.py:154
  122.1 10.6 %shard_map.68 = (bf16[2,64,128]{2,1,0:T(8,128)(2,1)S(1)}, bf16[256,8192]{1,0:T(8,128)(2,1)}) custom-call(s32[128]{0:T(128)S(1)} %reshape.320.refs_0_, s32[128]{0:T(128)S(1)} %reshape.315.refs_1_.refs_0_, s32[4]{0:T(128)S(1)} %fusion.13.refs_2_.refs_1_, s32[1]{0:T(128)} %bitcast.8.refs_3_.refs_2_, bf16[32,2,64,128]{3,2,1,0:T(8,128)(2,1)S(1)} %bitcast.39, ...), custom_call_target="tpu_custom_call" | custom-call | tf_op jit(solution)/shard_map/pallas_call | solution.py:184
  132.7 0.1 broadcast_in_dim.72
  132.8 24.7 %all_to_all.26.refs_4_ = bf16[16,128,128]{2,1,0:T(8,128)(2,1)S(1)} all-to-all(bf16[16,128,128]{2,1,0:T(8,128)(2,1)S(1)} %broadcast_in_dim.72), channel_id=1, replica_groups={{0,64,128,192,256,320,384,448,512,576,640,704,768,832,896,960},{32,96,1..., dimensions={0} | all-to-all | bytes 1048576 | tf_op jit(solution)/shard_map/all_to_all | solution.py:164
  157.5 2.9 %collective-permute-start.1 = (bf16[16,128,128]{2,1,0:T(8,128)(2,1)S(1)}, bf16[16,128,128]{2,1,0:T(8,128)(2,1)S(1)}, u32[]{:S(2)}, u32[]{:S(2)}) collective-permute-start(bf16[16,128,128]{2,1,0:T(8,128)(2,1)S(1)} %all_to_all.26.refs_4_), channel_id=1, source_target_pairs={{0,32},{32,0},{64,96},{96,64},{128,160},{160,128},{192,224},{224,1... | collective-permute-start | bytes 1572872 | tf_op jit(solution)/shard_map/ppermute | solution.py:168
  160.5 0.1 reshape.318
  160.6 0.7 broadcast_in_dim_reshape.8
  161.3 0.7 collective-permute-done.1.refs_5_
  162.0 0.0 copy-start
  162.0 2.2 %copy-done = bf16[256,8192]{1,0:T(8,128)(2,1)S(1)} copy-done((bf16[256,8192]{1,0:T(8,128)(2,1)S(1)}, bf16[256,8192]{1,0:T(8,128)(2,1)}, u32[]{:S(2)}) %copy-start) | copy-done | bytes 4194328
  164.2 5.2 %shard_map.69 = bf16[2,64,128]{2,1,0:T(8,128)(2,1)S(1)} custom-call(s32[128]{0:T(128)S(1)} %reshape.315.refs_1_.refs_0_, s32[4]{0:T(128)S(1)} %fusion.13.refs_2_.refs_1_, s32[1]{0:T(128)} %bitcast.8.refs_3_.refs_2_, bf16[256,8192]{1,0:T(8,128)(2,1)S(1)} %copy-done, bf16[16,128,128]{2,1,0:T(8,128)(2,1)S(1)} %all_to_all.26.refs_4_, ...), custom_call_target="tpu_custom_call" | custom-call | tf_op jit(solution)/shard_map/pallas_call | solution.py:197
  169.4 0.1 reshape.319
  169.5 0.7 broadcast_in_dim_reshape.9
  (9 shorter events, 0.1 us)
Async XLA Ops:
  0.6 37.6 %copy-start.2 = (s32[1,4]{1,0:T(1,128)S(1)}, s32[1,4]{1,0:T(1,128)}, u32[]{:S(2)}) copy-start(s32[1,4]{1,0:T(1,128)} %param.8) | copy-start | bytes 52
  0.6 31.4 %copy-start.1 = (bf16[1,4,4096]{2,1,0:T(4,128)(2,1)S(1)}, bf16[1,4,4096]{2,1,0:T(4,128)(2,1)}, u32[]{:S(2)}) copy-start(bf16[1,4,4096]{2,1,0:T(4,128)(2,1)} %param.7) | copy-start | bytes 98308
  8.5 22.1 %all-to-all-start = ((bf16[32,2,4224]{2,1,0:T(2,128)(2,1)}), bf16[32,2,4224]{2,1,0:T(2,128)(2,1)S(1)}, u32[]{:S(2)}, u32[]{:S(2)}) async-start(bf16[32,2,4224]{2,1,0:T(2,128)(2,1)} %concatenate.12), calls=%async_computation | async-start | bytes 1081344 | tf_op jit(solution)/shard_map/all_to_all | solution.py:139
  33.2 9.2 %all-to-all-start.2 = ((bf16[4,2,64,128]{3,2,1,0:T(8,128)(2,1)}), bf16[4,2,64,128]{3,2,1,0:T(8,128)(2,1)S(1)}, u32[]{:S(2)}, u32[]{:S(2)}) async-start(bf16[4,2,64,128]{3,2,1,0:T(8,128)(2,1)} %broadcast_in_dim.69), calls=%async_computation.2 | async-start | bytes 262144 | tf_op jit(solution)/shard_map/all_to_all | solution.py:150
  89.2 33.0 %all-to-all-start.3 = ((bf16[8,4,2,64,128]{4,3,2,1,0:T(8,128)(2,1)}), bf16[8,4,2,64,128]{4,3,2,1,0:T(8,128)(2,1)S(1)}, u32[]{:S(2)}, u32[]{:S(2)}) async-start(bf16[8,4,2,64,128]{4,3,2,1,0:T(8,128)(2,1)} %broadcast_in_dim.70), calls=%async_computation.3 | async-start | bytes 2097152 | tf_op jit(solution)/shard_map/all_to_all | solution.py:154
  92.9 5.7 %collective-permute-start = (bf16[16,144,128]{2,1,0:T(8,128)(2,1)S(1)}, bf16[16,144,128]{2,1,0:T(8,128)(2,1)S(1)}, u32[]{:S(2)}, u32[]{:S(2)}) collective-permute-start(bf16[16,144,128]{2,1,0:T(8,128)(2,1)S(1)} %all_to_all.25.refs_5_), channel_id=1, source_target_pairs={{0,32},{32,0},{64,96},{96,64},{128,160},{160,128},{192,224},{224,1... | collective-permute-start | bytes 1769480 | tf_op jit(solution)/shard_map/ppermute | solution.py:168
  157.5 4.5 %collective-permute-start.1 = (bf16[16,128,128]{2,1,0:T(8,128)(2,1)S(1)}, bf16[16,128,128]{2,1,0:T(8,128)(2,1)S(1)}, u32[]{:S(2)}, u32[]{:S(2)}) collective-permute-start(bf16[16,128,128]{2,1,0:T(8,128)(2,1)S(1)} %all_to_all.26.refs_4_), channel_id=1, source_target_pairs={{0,32},{32,0},{64,96},{96,64},{128,160},{160,128},{192,224},{224,1... | collective-permute-start | bytes 1572872 | tf_op jit(solution)/shard_map/ppermute | solution.py:168
  162.0 2.2 %copy-start = (bf16[256,8192]{1,0:T(8,128)(2,1)S(1)}, bf16[256,8192]{1,0:T(8,128)(2,1)}, u32[]{:S(2)}) copy-start(bf16[256,8192]{1,0:T(8,128)(2,1)} %get-tuple-element.17.refs_3_) | copy-start | bytes 12582916

commit v2 on v0

v2 whole, which is shorter than its diff:
```python
import math

import jax
import jax.numpy as jnp
from jax import lax
from jax.experimental import pallas as pl
from jax.experimental.pallas import tpu as pltpu
from jax.sharding import PartitionSpec as P

BS = 64
SLOTS = 4
SIDE = 4
TILE = BS * SIDE
LANES = 2 * BS
VMEM = pl.BlockSpec(memory_space=pltpu.VMEM)
SMEM = pl.BlockSpec(memory_space=pltpu.SMEM)
ANY = pl.BlockSpec(memory_space=pl.ANY)
BF16 = jnp.bfloat16
F32 = jnp.float32
I32 = jnp.int32


def params(megabytes):
    return pltpu.CompilerParams(vmem_limit_bytes=megabytes * 1024 * 1024)


def cost(flops, megabytes):
    return pl.CostEstimate(flops=flops, bytes_accessed=megabytes * 1024 * 1024, transcendentals=0)


def pack(blocks):
    return blocks.reshape(2, 2, BS, BS).transpose(0, 2, 1, 3).reshape(2, BS, LANES)


def unpack(pairs):
    return pairs.reshape(2, BS, 2, BS).transpose(0, 2, 1, 3).reshape(SLOTS, BS * BS)


def swap_halves(x):
    return jnp.concatenate([x[:, BS:], x[:, :BS]], axis=1)


def place_pair(dense, row, column, pair, spots, fresh):
    lane = lax.broadcasted_iota(I32, (1, LANES), 1)
    low = jnp.where(lane < BS, 1.0, 0.0).astype(BF16)
    high = jnp.where(lane < BS, 0.0, 1.0).astype(BF16)
    swapped = swap_halves(pair)
    for slot, spot in enumerate(spots):
        half = spot & 1
        block = jnp.where(half == slot, pair, swapped) * jnp.where(half == 0, low, high)
        rows = pl.ds(pl.multiple_of(row + (spot >> 2) * BS, BS), BS)
        columns = pl.ds(pl.multiple_of(column + ((spot & 3) >> 1) * LANES, LANES), LANES)
        if fresh and slot == 0:
            dense[rows, columns] = block
        else:
            dense[rows, columns] = dense[rows, columns] + block


def payload_kernel(places_per, count, words, blocks, payload):
    shift = count.bit_length() - 1
    width = blocks.shape[-1]
    items = payload.shape[0] * places_per
    payload[:, :, :width] = blocks[...]
    lane = lax.broadcasted_iota(I32, (1, LANES), 1)
    base = jnp.zeros((1, LANES), I32)
    for slot in range(SLOTS):
        code = words[items + count + slot]
        spot = ((code >> shift) & (SIDE - 1)) * SIDE + (code & (SIDE - 1))
        base = jnp.where(lane == 1 + slot, spot, base)

    def body(j, carry):
        rows = []
        for k in range(places_per):
            task = words[j * places_per + k]
            safe = jnp.maximum(task, 0)
            block_row = words[items + (safe >> shift)] & (SIDE - 1)
            block_column = words[items + (safe & (count - 1))] & (SIDE - 1)
            spot = jnp.where(task < 0, -1, block_row * SIDE + block_column)
            rows.append(jnp.where(lane == 0, spot, base))
        payload[j, :, width:] = jnp.concatenate(rows, axis=0).astype(F32).astype(BF16)
        return carry

    lax.fori_loop(0, payload.shape[0], body, 0, unroll=4)


def left_kernel(codes, core, panel, dense, work, sems):
    copies = []
    for half in range(2):
        work[half] = jnp.zeros(work.shape[1:], work.dtype)

        def body(u, carry, half=half):
            t = 2 * u + (core[0] ^ half)
            for pair in range(2):
                at = t * SLOTS + 2 * pair
                spots = (codes[at], codes[at + 1])
                place_pair(work.at[half], 0, u * TILE, panel[t, pair], spots, pair == 0)
            return carry

        lax.fori_loop(0, panel.shape[0] // 2, body, 0, unroll=4)
        copies.append(pltpu.make_async_copy(work.at[half], dense.at[half], sems.at[half]))
        copies[half].start()
    for copy in copies:
        copy.wait()


def partial_product(codes, first_code, source, left, which, panel, right, left_half, sem):
    copy = pltpu.make_async_copy(left.at[which], left_half, sem)
    copy.start()
    right[...] = jnp.zeros_like(right)

    def body(e, carry):
        row = source(e) * TILE
        for pair in range(2):
            at = e * 2 * SLOTS + first_code + 2 * pair
            data = panel[e, pair * BS : (pair + 1) * BS, :]
            place_pair(right, row, 0, data, (codes[at], codes[at + 1]), pair == 0)
        return carry

    lax.fori_loop(0, panel.shape[0], body, 0, unroll=4)
    copy.wait()
    return jnp.dot(left_half[...], right[...], preferred_element_type=F32)


def source_of(flipped, chip):
    return (lambda e: e ^ (chip & 1)) if flipped else lambda e: e


def own_pairs(total, own):
    lane = lax.broadcasted_iota(I32, (BS, LANES), 1)
    pairs = []
    for pair in range(2):
        parts = []
        for slot in (2 * pair, 2 * pair + 1):
            spot = own[slot]
            rows = pl.ds(pl.multiple_of((spot // SIDE) * BS, BS), BS)
            columns = pl.ds(pl.multiple_of(((spot % SIDE) // 2) * LANES, LANES), LANES)
            block = total[rows, columns]
            parts.append(jnp.where(spot % 2 == slot % 2, block, pltpu.roll(block, BS, 1)))
        pairs.append(jnp.where(lane < BS, parts[0], parts[1]))
    return pairs


def first_half_kernel(flipped, codes, chip, left, panel, total, *scratch):
    source = source_of(flipped, chip[0])
    total[...] = partial_product(codes, 0, source, left, 0, panel, *scratch)


def finish(flipped, codes, chip, own, left, panel, before, total, *scratch):
    source = source_of(flipped, chip[0])
    total[...] = before[...] + partial_product(
        codes, SLOTS, source, left, 1, panel, *scratch
    )
    return own_pairs(total, own)


def square_kernel(scale, codes, chip, own, left, panel, before, square, codes_by_chip, *scratch):
    source = source_of(True, chip[0])

    def body(e, carry):
        for slot in range(2 * SLOTS):
            codes_by_chip[source(e) * 2 * SLOTS + slot] = codes[e * 2 * SLOTS + slot]
        return carry

    lax.fori_loop(0, panel.shape[0], body, 0)
    for pair, value in enumerate(finish(True, codes, chip, own, left, panel, before, *scratch)):
        square[pair] = (scale * value).astype(square.dtype)


def sign_kernel(scale, codes, chip, own, left, panel, before, matrix, sign_next, *scratch):
    for pair, value in enumerate(finish(False, codes, chip, own, left, panel, before, *scratch)):
        old = matrix[pair].astype(F32)
        sign_next[pair] = (1.5 * old - 0.5 * scale * value).astype(sign_next.dtype)


def local(matrix_blocks, block_codes, block_perm, grid_blocks, grid_tasks):
    col_count = lax.axis_size("col")
    row_count = lax.axis_size("row")
    chips = row_count // 2
    block_count = block_perm.shape[0]
    barrier = lax.optimization_barrier
    row = lax.axis_index("row")
    core_word = (row % 2).astype(I32).reshape(1)
    chip_word = (row // 2).astype(I32).reshape(1)
    own_codes = block_codes[0]
    own_place = (own_codes // block_count) % SIDE * SIDE + own_codes % SIDE

    def permute(x, mask):
        return lax.ppermute(x, "row", [(i, i ^ mask) for i in range(row_count)])

    cap = grid_tasks.shape[1] // col_count
    width = grid_blocks.shape[-1]
    words = jnp.concatenate([grid_tasks[0], block_perm, own_codes])
    payload = pl.pallas_call(
        lambda *refs: payload_kernel(cap, block_count, *refs),
        out_shape=jax.ShapeDtypeStruct((col_count, cap, width + LANES), BF16),
        in_specs=[SMEM, VMEM],
        out_specs=VMEM,
        compiler_params=params(8),
    )(words, grid_blocks[0].reshape(col_count, cap, width))
    received = lax.all_to_all(payload, "col", 0, 0, tiled=True)
    partner_place = permute(own_place, 1)
    codes_left = received[:, 0, width + 1 : width + 1 + SLOTS].astype(I32).reshape(-1)
    arrived_place = received[:, :, width].astype(I32).reshape(-1)
    items = received.reshape(-1, width + LANES)
    matches = (own_place[:, None] == arrived_place[None, :]).astype(BF16)
    grid_sum = jnp.dot(matches, items, preferred_element_type=F32)[:, :width]
    matrix = (matrix_blocks[0].astype(F32) + grid_sum).astype(BF16)
    pairs = barrier(pack(matrix))

    rows = pairs.reshape(2 * BS, LANES)
    panel = lax.all_to_all(
        jnp.broadcast_to(rows[None], (col_count,) + rows.shape), "col", 0, 0, tiled=True
    ).reshape((col_count,) + pairs.shape)
    chip_codes = jnp.concatenate([own_place, partner_place]).astype(BF16)
    code_rows = jnp.zeros((16, LANES), BF16).at[0, : 2 * SLOTS].set(chip_codes)
    tile = jnp.concatenate([rows, code_rows], axis=0)
    both = jnp.stack([tile, permute(tile, 2)])
    panel, both = barrier((panel, both))
    half_shape = (TILE, col_count // 2 * TILE)
    left = pl.pallas_call(
        left_kernel,
        out_shape=jax.ShapeDtypeStruct((10,) + half_shape, BF16),
        in_specs=[SMEM] * 2 + [VMEM],
        out_specs=ANY,
        scratch_shapes=[pltpu.VMEM((2,) + half_shape, BF16), pltpu.SemaphoreType.DMA((2,))],
        compiler_params=params(48),
        cost_estimate=cost(1 << 32, 8),
    )(codes_left, core_word, panel)
    lines = [[4 * z + k for z in range(row_count // 4)] for k in range(4)]
    mine = lax.all_to_all(
        jnp.broadcast_to(both[None], (row_count // 4,) + both.shape),
        "row", 0, 0, axis_index_groups=lines, tiled=True,
    ).reshape((chips,) + tile.shape)
    mine, left = barrier((mine, left))
    codes_right = mine[:, 2 * BS, : 2 * SLOTS].astype(I32).reshape(-1)
    other = permute(mine, 1)

    scale = 1.5 / math.sqrt(BS * SLOTS * col_count / (block_count // row_count))
    depth = col_count * TILE
    total_shape = jax.ShapeDtypeStruct((TILE, TILE), F32)
    tile_shape = jax.ShapeDtypeStruct(pairs.shape, BF16)
    work = [
        pltpu.VMEM((depth // 2, TILE), BF16),
        pltpu.VMEM((TILE, depth // 2), BF16),
        pltpu.SemaphoreType.DMA,
    ]
    settings = dict(
        compiler_params=params(48), cost_estimate=cost(2 * TILE * TILE * depth // 2, 6)
    )

    def first_half(flipped, codes, mine):
        return pl.pallas_call(
            lambda *refs: first_half_kernel(flipped, *refs),
            out_shape=total_shape,
            in_specs=[SMEM] * 2 + [ANY, VMEM],
            out_specs=VMEM,
            scratch_shapes=work,
            **settings,
        )(codes, chip_word, left, mine)

    before = first_half(True, codes_right, mine)
    square, codes_by_chip = pl.pallas_call(
        lambda *refs: square_kernel(scale, *refs),
        out_shape=(tile_shape, jax.ShapeDtypeStruct(codes_right.shape, I32)),
        in_specs=[SMEM] * 3 + [ANY] + [VMEM] * 2,
        out_specs=(VMEM, SMEM),
        scratch_shapes=[pltpu.VMEM((TILE, TILE), F32)] + work,
        **settings,
    )(codes_right, chip_word, own_place, left, other, before)

    cores = [[2 * chip + one for chip in range(chips)] for one in range(2)]
    rows = square.reshape(2 * BS, LANES)
    mine = lax.all_to_all(
        jnp.broadcast_to(rows[None], (chips,) + rows.shape),
        "row", 0, 0, axis_index_groups=cores, tiled=True,
    )
    square_out = unpack(square)[None]
    mine, square_out = barrier((mine, square_out))
    other = permute(mine, 1)
    before = first_half(False, codes_by_chip, mine)
    sign_next = pl.pallas_call(
        lambda *refs: sign_kernel(scale, *refs),
        out_shape=tile_shape,
        in_specs=[SMEM] * 3 + [ANY] + [VMEM] * 3,
        out_specs=VMEM,
        scratch_shapes=[pltpu.VMEM((TILE, TILE), F32)] + work,
        **settings,
    )(codes_by_chip, chip_word, own_place, left, other, before, pairs)
    return (square_out, unpack(sign_next)[None])


def solution(mesh):
    in_specs = (P("row", "col", None), P("row", "col"), P(), P("row", "col", None), P("row", "col"))
    out_specs = (P("row", "col", None), P("row", "col", None))
    return jax.shard_map(local, mesh=mesh, in_specs=in_specs, out_specs=out_specs, check_vma=False)
```

time: 436 us -> 151 us (0.35)
  the two profiles are of different devices: /device:TPU:1 before, /device:TPU:33 now
where the time goes in v2:
time: 151 us
  starting transfers between devices  68.8 us (46%)
  waiting for transfers between devices  52.4 us (35%)
  Pallas kernels  17.6 us (12%)
  local copies, waits for them, and re-layouts  6.85 us (5%)
  other arithmetic  2.99 us (2%)
    all_to_all x1, starting transfers between devices, local(): lax.all_to_all(jnp.broadcast_to(both[None], (row_count // 4,) + both.shap...  26.8 us
    ppermute x4, starting transfers between devices, permute(): return lax.ppermute(x, 'row', [(i, i ^ mask) for i in range(row_count)])  22.2 us
    all_to_all x1, waiting for transfers between devices, local(): lax.all_to_all(jnp.broadcast_to(rows[None], (chips,) + rows.shape), 'row'...  20.4 us
    all_to_all x1, waiting for transfers between devices, local(): lax.all_to_all(jnp.broadcast_to(both[None], (row_count // 4,) + both.shap...  13 us
    all_to_all x1, waiting for transfers between devices, local(): received = lax.all_to_all(payload, 'col', 0, 0, tiled=True)  11.3 us
    all_to_all x1, starting transfers between devices, local(): received = lax.all_to_all(payload, 'col', 0, 0, tiled=True)  9.84 us
    ppermute x4, waiting for transfers between devices, permute(): return lax.ppermute(x, 'row', [(i, i ^ mask) for i in range(row_count)])  7.71 us
    pallas_call x2, Pallas kernels, first_half(): pl.pallas_call(lambda *refs: first_half_kernel(flipped, *refs), out_shape...  5.7 us
  transfers between devices with their start and end apart: 8, of which 5 were waited for; matrix products, arithmetic and copies ran while one was open for 2% of the time, Pallas kernels for 6%

profile of v2, /device:TPU:33, one launch (start us, length us, event | category | flops | bytes accessed | tf_op | source)
XLA Modules:
  0.0 150.5 jit_solution(12318269543074958388)
XLA Ops:
  0.6 1.4 reshape_squeeze.3.refs_1_
  2.0 0.8 pad_add_fusion.refs_0_
  2.8 1.7 %shard_map.68 = bf16[32,2,4224]{2,1,0:T(2,128)(2,1)} custom-call(s32[196]{0:T(256)S(1)} %pad_add_fusion.refs_0_, bf16[32,2,4096]{2,1,0:T(2,128)(2,1)S(1)} %reshape_squeeze.3.refs_1_), custom_call_target="tpu_custom_call" | custom-call | tf_op jit(solution)/shard_map/pallas_call | solution.py:193
  4.5 9.8 %all-to-all-start = ((bf16[32,2,4224]{2,1,0:T(2,128)(2,1)}), bf16[32,2,4224]{2,1,0:T(2,128)(2,1)S(1)}, u32[]{:S(2)}, u32[]{:S(2)}) async-start(bf16[32,2,4224]{2,1,0:T(2,128)(2,1)} %shard_map.68), calls=%async_computation | async-start | bytes 1081344 | tf_op jit(solution)/shard_map/all_to_all | solution.py:200
  14.4 0.7 fusion.12.refs_2_
  15.0 11.3 %all-to-all-done = bf16[32,2,4224]{2,1,0:T(2,128)(2,1)S(1)} async-done(((bf16[32,2,4224]{2,1,0:T(2,128)(2,1)}), bf16[32,2,4224]{2,1,0:T(2,128)(2,1)S(1)}, u32[]{:S(2)}, u32[]{:S(2)}) %all-to-all-start) | async-done | bytes 540704 | tf_op jit(solution)/shard_map/all_to_all | solution.py:200
  26.3 0.6 convert_reduce_fusion
  26.9 0.1 reshape.170
  27.0 0.2 reshape.160
  27.3 1.0 fusion
  28.3 0.1 reshape.161
  28.4 0.1 copy.14
  28.5 0.1 reshape.162.refs_6_
  28.6 1.2 broadcast_in_dim.11
  29.8 5.3 %all-to-all-start.1 = ((bf16[32,128,128]{2,1,0:T(8,128)(2,1)}), bf16[32,128,128]{2,1,0:T(8,128)(2,1)S(1)}, u32[]{:S(2)}, u32[]{:S(2)}) async-start(bf16[32,128,128]{2,1,0:T(8,128)(2,1)} %broadcast_in_dim.11), calls=%async_computation.1 | async-start | bytes 2097152 | tf_op jit(solution)/shard_map/all_to_all | solution.py:211
  35.1 10.2 %collective-permute-start = (s32[4]{0:T(128)S(1)}, s32[4]{0:T(128)S(1)}, u32[]{:S(2)}, u32[]{:S(2)}) collective-permute-start(s32[4]{0:T(128)S(1)} %fusion.12.refs_2_), channel_id=1, source_target_pairs={{0,32},{32,0},{64,96},{96,64},{128,160},{160,128},{192,224},{224,1... | collective-permute-start | bytes 56 | tf_op jit(solution)/shard_map/ppermute | solution.py:188
  45.3 0.7 fusion.18
  46.0 0.1 collective-permute-done
  46.1 0.1 fusion.8
  46.2 3.4 %collective-permute-start.1 = (bf16[144,128]{1,0:T(8,128)(2,1)S(1)}, bf16[144,128]{1,0:T(8,128)(2,1)S(1)}, u32[]{:S(2)}, u32[]{:S(2)}) collective-permute-start(bf16[144,128]{1,0:T(8,128)(2,1)S(1)} %get-tuple-element.31), channel_id=1, source_target_pairs={{0,64},{32,96},{64,0},{96,32},{128,192},{160,224},{192,128},{224,1... | collective-permute-start | bytes 110600 | tf_op jit(solution)/shard_map/ppermute | solution.py:188
  49.6 7.6 %collective-permute-done.1 = bf16[144,128]{1,0:T(8,128)(2,1)S(1)} collective-permute-done((bf16[144,128]{1,0:T(8,128)(2,1)S(1)}, bf16[144,128]{1,0:T(8,128)(2,1)S(1)}, u32[]{:S(2)}, u32[]{:S(2)}) %collective-permute-start.1) | collective-permute-done | bytes 36896 | tf_op jit(solution)/shard_map/ppermute | solution.py:188
  57.2 0.0 all-to-all-done.1
  57.2 0.9 broadcast_in_dim.24
  58.1 26.8 %all-to-all-start.2 = ((bf16[8,2,144,128]{3,2,1,0:T(8,128)(2,1)}), bf16[8,2,144,128]{3,2,1,0:T(8,128)(2,1)S(1)}, u32[]{:S(2)}, u32[]{:S(2)}) async-start(bf16[8,2,144,128]{3,2,1,0:T(8,128)(2,1)} %broadcast_in_dim.24), calls=%async_computation.2 | async-start | bytes 1179648 | tf_op jit(solution)/shard_map/all_to_all | solution.py:230
  84.9 0.1 fusion.2
  85.0 0.1 reshape.171.codes
  85.1 3.6 %shard_map.69.refs_2_.refs_3_ = bf16[10,256,4096]{2,1,0:T(8,128)(2,1)} custom-call(s32[128]{0:T(128)S(1)} %reshape.171.codes, s32[1]{0:T(128)} %bitcast.10.core, bf16[32,2,64,128]{3,2,1,0:T(8,128)(2,1)S(1)} %bitcast.26), custom_call_target="tpu_custom_call" | custom-call | flops 4294967296 | bytes 8388608 | tf_op jit(solution)/shard_map/pallas_call | solution.py:220
  88.7 13.0 %all-to-all-done.2 = bf16[8,2,144,128]{3,2,1,0:T(8,128)(2,1)S(1)} async-done(((bf16[8,2,144,128]{3,2,1,0:T(8,128)(2,1)}), bf16[8,2,144,128]{3,2,1,0:T(8,128)(2,1)S(1)}, u32[]{:S(2)}, u32[]{:S(2)}) %all-to-all-start.2) | async-done | bytes 589856 | tf_op jit(solution)/shard_map/all_to_all | solution.py:230
  101.7 4.9 %collective-permute-start.2 = (bf16[16,144,128]{2,1,0:T(8,128)(2,1)S(1)}, bf16[16,144,128]{2,1,0:T(8,128)(2,1)S(1)}, u32[]{:S(2)}, u32[]{:S(2)}) collective-permute-start(bf16[16,144,128]{2,1,0:T(8,128)(2,1)S(1)} %bitcast.27), channel_id=1, source_target_pairs={{0,32},{32,0},{64,96},{96,64},{128,160},{160,128},{192,224},{224,1... | collective-permute-start | bytes 1769480 | tf_op jit(solution)/shard_map/ppermute | solution.py:188
  106.7 0.1 reshape.172.refs_0_
  106.8 2.9 %shard_map.70.refs_5_ = f32[256,256]{1,0:T(8,128)S(1)} custom-call(s32[128]{0:T(128)S(1)} %reshape.172.refs_0_, s32[1]{0:T(128)} %bitcast.11.refs_1_, bf16[10,256,4096]{2,1,0:T(8,128)(2,1)} %shard_map.69.refs_2_.refs_3_, bf16[16,144,128]{2,1,0:T(8,128)(2,1)S(1)} %bitcast.29), custom_call_target="tpu_custom_call" | custom-call | flops 536870912 | bytes 6291456 | tf_op jit(solution)/shard_map/pallas_call | solution.py:252
  109.6 0.0 collective-permute-done.2.refs_4_
  109.6 3.7 %shard_map.71 = (bf16[2,64,128]{2,1,0:T(8,128)(2,1)S(1)}, s32[128]{0:T(128)S(1)}) custom-call(s32[128]{0:T(128)S(1)} %reshape.172.refs_0_, s32[1]{0:T(128)} %bitcast.11.refs_1_, s32[4]{0:T(128)S(1)} %fusion.12.refs_2_, bf16[10,256,4096]{2,1,0:T(8,128)(2,1)} %shard_map.69.refs_2_.refs_3_, bf16[16,144,128]{2,1,0:T(8,128)(2,1)S(1)} %collective-permute-done.2.refs_4_, ...), custom_call_target="tpu_custom_call" | custom-call | flops 536870912 | bytes 6291456 | tf_op jit(solution)/shard_map/pallas_call | solution.py:262
  113.3 0.9 broadcast_in_dim.26
  114.2 4.7 %all-to-all-start.3 = ((bf16[16,128,128]{2,1,0:T(8,128)(2,1)}), bf16[16,128,128]{2,1,0:T(8,128)(2,1)S(1)}, u32[]{:S(2)}, u32[]{:S(2)}) async-start(bf16[16,128,128]{2,1,0:T(8,128)(2,1)} %broadcast_in_dim.26), calls=%async_computation.3 | async-start | bytes 1048576 | tf_op jit(solution)/shard_map/all_to_all | solution.py:273
  118.9 0.1 reshape.167
  119.0 0.7 broadcast_in_dim_reshape.4
  119.8 20.4 %all-to-all-done.3.refs_3_ = bf16[16,128,128]{2,1,0:T(8,128)(2,1)S(1)} async-done(((bf16[16,128,128]{2,1,0:T(8,128)(2,1)}), bf16[16,128,128]{2,1,0:T(8,128)(2,1)S(1)}, u32[]{:S(2)}, u32[]{:S(2)}) %all-to-all-start.3) | async-done | bytes 524320 | tf_op jit(solution)/shard_map/all_to_all | solution.py:273
  140.2 3.7 %collective-permute-start.3 = (bf16[16,128,128]{2,1,0:T(8,128)(2,1)S(1)}, bf16[16,128,128]{2,1,0:T(8,128)(2,1)S(1)}, u32[]{:S(2)}, u32[]{:S(2)}) collective-permute-start(bf16[16,128,128]{2,1,0:T(8,128)(2,1)S(1)} %all-to-all-done.3.refs_3_), channel_id=1, source_target_pairs={{0,32},{32,0},{64,96},{96,64},{128,160},{160,128},{192,224},{224,1... | collective-permute-start | bytes 1572872 | tf_op jit(solution)/shard_map/ppermute | solution.py:188
  143.8 2.9 %shard_map.72.refs_5_ = f32[256,256]{1,0:T(8,128)S(1)} custom-call(s32[128]{0:T(128)S(1)} %get-tuple-element.28.refs_0_, s32[1]{0:T(128)} %bitcast.11.refs_1_, bf16[10,256,4096]{2,1,0:T(8,128)(2,1)} %shard_map.69.refs_2_.refs_3_, bf16[16,128,128]{2,1,0:T(8,128)(2,1)S(1)} %all-to-all-done.3.refs_3_), custom_call_target="tpu_custom_call" | custom-call | flops 536870912 | bytes 6291456 | tf_op jit(solution)/shard_map/pallas_call | solution.py:252
  146.7 0.0 collective-permute-done.3.refs_4_
  146.7 3.0 %shard_map.73 = bf16[2,64,128]{2,1,0:T(8,128)(2,1)S(1)} custom-call(s32[128]{0:T(128)S(1)} %get-tuple-element.28.refs_0_, s32[1]{0:T(128)} %bitcast.11.refs_1_, s32[4]{0:T(128)S(1)} %fusion.12.refs_2_, bf16[10,256,4096]{2,1,0:T(8,128)(2,1)} %shard_map.69.refs_2_.refs_3_, bf16[16,128,128]{2,1,0:T(8,128)(2,1)S(1)} %collective-permute-done.3.refs_4_, ...), custom_call_target="tpu_custom_call" | custom-call | flops 536870912 | bytes 6291456 | tf_op jit(solution)/shard_map/pallas_call | solution.py:281
  149.7 0.1 reshape.168
  149.8 0.7 broadcast_in_dim_reshape.10
  (6 shorter events, 0.1 us)
Async XLA Ops:
  4.5 21.8 %all-to-all-start = ((bf16[32,2,4224]{2,1,0:T(2,128)(2,1)}), bf16[32,2,4224]{2,1,0:T(2,128)(2,1)S(1)}, u32[]{:S(2)}, u32[]{:S(2)}) async-start(bf16[32,2,4224]{2,1,0:T(2,128)(2,1)} %shard_map.68), calls=%async_computation | async-start | bytes 1081344 | tf_op jit(solution)/shard_map/all_to_all | solution.py:200
  29.8 27.4 %all-to-all-start.1 = ((bf16[32,128,128]{2,1,0:T(8,128)(2,1)}), bf16[32,128,128]{2,1,0:T(8,128)(2,1)S(1)}, u32[]{:S(2)}, u32[]{:S(2)}) async-start(bf16[32,128,128]{2,1,0:T(8,128)(2,1)} %broadcast_in_dim.11), calls=%async_computation.1 | async-start | bytes 2097152 | tf_op jit(solution)/shard_map/all_to_all | solution.py:211
  35.1 11.0 %collective-permute-start = (s32[4]{0:T(128)S(1)}, s32[4]{0:T(128)S(1)}, u32[]{:S(2)}, u32[]{:S(2)}) collective-permute-start(s32[4]{0:T(128)S(1)} %fusion.12.refs_2_), channel_id=1, source_target_pairs={{0,32},{32,0},{64,96},{96,64},{128,160},{160,128},{192,224},{224,1... | collective-permute-start | bytes 56 | tf_op jit(solution)/shard_map/ppermute | solution.py:188
  46.2 11.0 %collective-permute-start.1 = (bf16[144,128]{1,0:T(8,128)(2,1)S(1)}, bf16[144,128]{1,0:T(8,128)(2,1)S(1)}, u32[]{:S(2)}, u32[]{:S(2)}) collective-permute-start(bf16[144,128]{1,0:T(8,128)(2,1)S(1)} %get-tuple-element.31), channel_id=1, source_target_pairs={{0,64},{32,96},{64,0},{96,32},{128,192},{160,224},{192,128},{224,1... | collective-permute-start | bytes 110600 | tf_op jit(solution)/shard_map/ppermute | solution.py:188
  58.1 43.6 %all-to-all-start.2 = ((bf16[8,2,144,128]{3,2,1,0:T(8,128)(2,1)}), bf16[8,2,144,128]{3,2,1,0:T(8,128)(2,1)S(1)}, u32[]{:S(2)}, u32[]{:S(2)}) async-start(bf16[8,2,144,128]{3,2,1,0:T(8,128)(2,1)} %broadcast_in_dim.24), calls=%async_computation.2 | async-start | bytes 1179648 | tf_op jit(solution)/shard_map/all_to_all | solution.py:230
  101.7 8.0 %collective-permute-start.2 = (bf16[16,144,128]{2,1,0:T(8,128)(2,1)S(1)}, bf16[16,144,128]{2,1,0:T(8,128)(2,1)S(1)}, u32[]{:S(2)}, u32[]{:S(2)}) collective-permute-start(bf16[16,144,128]{2,1,0:T(8,128)(2,1)S(1)} %bitcast.27), channel_id=1, source_target_pairs={{0,32},{32,0},{64,96},{96,64},{128,160},{160,128},{192,224},{224,1... | collective-permute-start | bytes 1769480 | tf_op jit(solution)/shard_map/ppermute | solution.py:188
  114.2 25.9 %all-to-all-start.3 = ((bf16[16,128,128]{2,1,0:T(8,128)(2,1)}), bf16[16,128,128]{2,1,0:T(8,128)(2,1)S(1)}, u32[]{:S(2)}, u32[]{:S(2)}) async-start(bf16[16,128,128]{2,1,0:T(8,128)(2,1)} %broadcast_in_dim.26), calls=%async_computation.3 | async-start | bytes 1048576 | tf_op jit(solution)/shard_map/all_to_all | solution.py:273
  140.2 6.5 %collective-permute-start.3 = (bf16[16,128,128]{2,1,0:T(8,128)(2,1)S(1)}, bf16[16,128,128]{2,1,0:T(8,128)(2,1)S(1)}, u32[]{:S(2)}, u32[]{:S(2)}) collective-permute-start(bf16[16,128,128]{2,1,0:T(8,128)(2,1)S(1)} %all-to-all-done.3.refs_3_), channel_id=1, source_target_pairs={{0,32},{32,0},{64,96},{96,64},{128,160},{160,128},{192,224},{224,1... | collective-permute-start | bytes 1572872 | tf_op jit(solution)/shard_map/ppermute | solution.py:188

commit v3 on v2

v3 whole, which is shorter than its diff:
```python
import math

import jax
import jax.numpy as jnp
from jax import lax
from jax.experimental import pallas as pl
from jax.experimental.pallas import tpu as pltpu
from jax.sharding import PartitionSpec as P

BS = 64
SLOTS = 4
SIDE = 4
TILE = BS * SIDE
LANES = 2 * BS
VMEM = pl.BlockSpec(memory_space=pltpu.VMEM)
SMEM = pl.BlockSpec(memory_space=pltpu.SMEM)
ANY = pl.BlockSpec(memory_space=pl.ANY)
BF16 = jnp.bfloat16
F32 = jnp.float32
I32 = jnp.int32


def params(megabytes):
    return pltpu.CompilerParams(vmem_limit_bytes=megabytes * 1024 * 1024)


def cost(flops, megabytes):
    return pl.CostEstimate(flops=flops, bytes_accessed=megabytes * 1024 * 1024, transcendentals=0)


def pack(blocks):
    return blocks.reshape(2, 2, BS, BS).transpose(0, 2, 1, 3).reshape(2, BS, LANES)


def unpack(pairs):
    return pairs.reshape(2, BS, 2, BS).transpose(0, 2, 1, 3).reshape(SLOTS, BS * BS)


def swap_halves(x):
    return jnp.concatenate([x[:, BS:], x[:, :BS]], axis=1)


def place_pair(dense, row, column, pair, spots, fresh):
    lane = lax.broadcasted_iota(I32, (1, LANES), 1)
    low = jnp.where(lane < BS, 1.0, 0.0).astype(BF16)
    high = jnp.where(lane < BS, 0.0, 1.0).astype(BF16)
    swapped = swap_halves(pair)
    for slot, spot in enumerate(spots):
        half = spot & 1
        block = jnp.where(half == slot, pair, swapped) * jnp.where(half == 0, low, high)
        rows = pl.ds(pl.multiple_of(row + (spot >> 2) * BS, BS), BS)
        columns = pl.ds(pl.multiple_of(column + ((spot & 3) >> 1) * LANES, LANES), LANES)
        if fresh and slot == 0:
            dense[rows, columns] = block
        else:
            dense[rows, columns] = dense[rows, columns] + block


def payload_kernel(places_per, count, words, blocks, payload):
    shift = count.bit_length() - 1
    width = blocks.shape[-1]
    items = payload.shape[0] * places_per
    for first in range(0, blocks.shape[0], 16):
        owners = pl.ds(first // places_per, 16 // places_per)
        payload[owners, :, :width] = blocks[first : first + 16].reshape(
            16 // places_per, places_per, width
        )
    lane = lax.broadcasted_iota(I32, (1, LANES), 1)
    base = jnp.zeros((1, LANES), I32)
    for slot in range(SLOTS):
        code = words[items + count + slot]
        spot = ((code >> shift) & (SIDE - 1)) * SIDE + (code & (SIDE - 1))
        base = jnp.where(lane == 1 + slot, spot, base)

    def body(j, carry):
        rows = []
        for k in range(places_per):
            task = words[j * places_per + k]
            safe = jnp.maximum(task, 0)
            block_row = words[items + (safe >> shift)] & (SIDE - 1)
            block_column = words[items + (safe & (count - 1))] & (SIDE - 1)
            spot = jnp.where(task < 0, -1, block_row * SIDE + block_column)
            rows.append(jnp.where(lane == 0, spot, base))
        payload[j, :, width:] = jnp.concatenate(rows, axis=0).astype(F32).astype(BF16)
        return carry

    lax.fori_loop(0, payload.shape[0], body, 0, unroll=8)


def spread_kernel(tile, copies, sems):
    sends = [
        pltpu.make_async_copy(tile, copies.at[k], sems.at[k]) for k in range(copies.shape[0])
    ]
    for send in sends:
        send.start()
    for send in sends:
        send.wait()


def spread(tile, count):
    return pl.pallas_call(
        spread_kernel,
        out_shape=jax.ShapeDtypeStruct((count,) + tile.shape, tile.dtype),
        in_specs=[VMEM],
        out_specs=ANY,
        scratch_shapes=[pltpu.SemaphoreType.DMA((count,))],
        compiler_params=params(8),
    )(tile)


def left_kernel(codes, partner_codes, place, panel, far, near, work, sem):
    core = place[0]
    count = panel.shape[0] // 4

    def fill(dense, first):
        dense[...] = jnp.zeros_like(dense)

        def body(v, carry):
            t = 2 * (first + v) + core
            for first_row, entry, source in ((0, t, codes), (TILE, t ^ 1, partner_codes)):
                for pair in range(2):
                    at = t * SLOTS + 2 * pair
                    spots = (source[at], source[at + 1])
                    place_pair(dense, first_row, v * TILE, panel[entry, pair], spots, pair == 0)
            return carry

        lax.fori_loop(0, count, body, 0, unroll=4)

    fill(work, count)
    copy = pltpu.make_async_copy(work, far.at[0], sem)
    copy.start()
    fill(near, 0)
    copy.wait()


def mirror(e):
    return (e & 5) | ((e & 2) << 2) | ((e & 8) >> 2)


def orders(doubled, chip):
    if doubled:
        return (lambda e: chip ^ mirror(e)), (lambda e: e)
    return (lambda e: e), (lambda e: mirror(e ^ chip))


def fill_right(doubled, codes, chip, panels, right):
    right[...] = jnp.zeros_like(right)
    slot, entry = orders(doubled, chip)
    first = 0
    for k, panel in enumerate(panels):

        def body(e, carry, first=first, panel=panel, codes=codes[k]):
            row = slot(first + e) * TILE
            for pair in range(2):
                at = (entry(first + e) - first) * SLOTS + 2 * pair
                data = panel[e, pair * BS : (pair + 1) * BS, :]
                place_pair(right, row, 0, data, (codes[at], codes[at + 1]), pair == 0)
            return carry

        lax.fori_loop(0, panel.shape[0], body, 0, unroll=4)
        first += panel.shape[0]


def own_pairs(total, first_row, own):
    lane = lax.broadcasted_iota(I32, (BS, LANES), 1)
    pairs = []
    for pair in range(2):
        parts = []
        for slot in (2 * pair, 2 * pair + 1):
            spot = own[slot]
            rows = pl.ds(pl.multiple_of(first_row + (spot >> 2) * BS, BS), BS)
            columns = pl.ds(pl.multiple_of(((spot & 3) >> 1) * LANES, LANES), LANES)
            block = total[rows, columns]
            parts.append(jnp.where(spot % 2 == slot % 2, block, pltpu.roll(block, BS, 1)))
        pairs.append(jnp.where(lane < BS, parts[0], parts[1]))
    return pairs


def product_kernel(doubled, count, place, own, theirs, far, near, *refs):
    codes, panels = refs[:count], refs[count : 2 * count]
    kept, sent, total, right, left, sem = refs[2 * count :]
    copy = pltpu.make_async_copy(far.at[0], left, sem)
    copy.start()
    fill_right(doubled, codes, place[1], panels, right)
    depth = near.shape[1]
    total[...] = jnp.dot(near[...], right[:depth], preferred_element_type=F32)
    copy.wait()
    total[...] += jnp.dot(left[...], right[depth:], preferred_element_type=F32)
    for out, first_row, spots in ((sent, TILE, theirs), (kept, 0, own)):
        for pair, value in enumerate(own_pairs(total, first_row, spots)):
            out[pair * BS : (pair + 1) * BS] = value


def square_kernel(scale, kept, received, square, copies, sems):
    square[...] = (scale * (kept[...] + received[...])).astype(square.dtype)
    spread_kernel(square, copies, sems)


def local(matrix_blocks, block_codes, block_perm, grid_blocks, grid_tasks):
    col_count = lax.axis_size("col")
    row_count = lax.axis_size("row")
    block_count = block_perm.shape[0]
    barrier = lax.optimization_barrier
    row = lax.axis_index("row")
    place = jnp.stack([row % 2, row // 2]).astype(I32)
    own_codes = block_codes[0]
    own_place = (own_codes // block_count) % SIDE * SIDE + own_codes % SIDE

    def permute(x, mask):
        return lax.ppermute(x, "row", [(i, i ^ mask) for i in range(row_count)])

    cap = grid_tasks.shape[1] // col_count
    width = grid_blocks.shape[-1]
    words = jnp.concatenate([grid_tasks[0], block_perm, own_codes])
    payload = pl.pallas_call(
        lambda *refs: payload_kernel(cap, block_count, *refs),
        out_shape=jax.ShapeDtypeStruct((col_count, cap, width + LANES), BF16),
        in_specs=[SMEM, VMEM],
        out_specs=VMEM,
        compiler_params=params(8),
    )(words, grid_blocks[0])
    received = lax.all_to_all(payload, "col", 0, 0, tiled=True)
    received, theirs = barrier((received, permute(own_place, 1)))
    codes_left = received[:, 0, width + 1 : width + 1 + SLOTS].astype(I32).reshape(-1)
    arrived_place = received[:, :, width].astype(I32).reshape(-1)
    items = received.reshape(-1, width + LANES)
    matches = (own_place[:, None] == arrived_place[None, :]).astype(BF16)
    grid_sum = jnp.dot(matches, items, preferred_element_type=F32)[:, :width]
    matrix = (matrix_blocks[0].astype(F32) + grid_sum).astype(BF16)
    pairs = barrier(pack(matrix))

    moves = []
    for r in range(row_count):
        for c in range(col_count):
            moves_on = (r ^ c) & 1
            target = (r ^ moves_on) * col_count + (c ^ moves_on)
            moves.append((r * col_count + c, target))
    rows = pairs.reshape(2 * BS, LANES)
    code_rows = jnp.zeros((8, LANES), BF16).at[0, :SLOTS].set(own_place.astype(BF16))
    tile = jnp.concatenate([rows, code_rows], axis=0)
    moved, across = barrier((lax.ppermute(rows, ("row", "col"), moves), permute(tile, 2)))

    panel = lax.all_to_all(spread(moved, col_count), "col", 0, 0, tiled=True).reshape(
        (col_count,) + pairs.shape
    )

    scale = 1.5 / math.sqrt(BS * SLOTS * col_count / (block_count // row_count))
    depth = col_count // 4 * TILE
    half_shape = (2 * TILE, depth)
    tile_shape = jax.ShapeDtypeStruct(rows.shape, F32)
    settings = dict(compiler_params=params(48), cost_estimate=cost(8 * TILE * TILE * depth, 6))
    gathered = jnp.stack([tile, across])
    for mask in (16, 8):
        gathered = jnp.concatenate([gathered, permute(gathered, mask)], axis=0)
    codes_left, gathered = barrier((codes_left, gathered))
    partner_codes = permute(codes_left, 1)
    far, near = pl.pallas_call(
        left_kernel,
        out_shape=(
            jax.ShapeDtypeStruct((10,) + half_shape, BF16),
            jax.ShapeDtypeStruct(half_shape, BF16),
        ),
        in_specs=[SMEM] * 3 + [VMEM],
        out_specs=(ANY, VMEM),
        scratch_shapes=[pltpu.VMEM(half_shape, BF16), pltpu.SemaphoreType.DMA],
        **settings,
    )(codes_left, partner_codes, place, panel)

    last, far, near = barrier((permute(gathered, 4), far, near))
    panels = [gathered, last]
    codes = [part[:, 2 * BS, :SLOTS].astype(I32).reshape(-1) for part in panels]

    def product(doubled, codes, panels):
        count = len(panels)
        kept, sent = pl.pallas_call(
            lambda *refs: product_kernel(doubled, count, *refs),
            out_shape=(tile_shape, tile_shape),
            in_specs=[SMEM] * 3 + [ANY, VMEM] + [SMEM] * count + [VMEM] * count,
            out_specs=(VMEM, VMEM),
            scratch_shapes=[
                pltpu.VMEM((2 * TILE, TILE), F32),
                pltpu.VMEM((2 * depth, TILE), BF16),
                pltpu.VMEM(half_shape, BF16),
                pltpu.SemaphoreType.DMA,
            ],
            **settings,
        )(place, own_place, theirs, far, near, *codes, *panels)
        return kept, permute(sent, 1)

    kept, received = product(True, codes, panels)
    chips = row_count // 2
    square, copies = pl.pallas_call(
        lambda *refs: square_kernel(scale, *refs),
        out_shape=(
            jax.ShapeDtypeStruct(rows.shape, BF16),
            jax.ShapeDtypeStruct((chips,) + rows.shape, BF16),
        ),
        in_specs=[VMEM] * 2,
        out_specs=(VMEM, ANY),
        scratch_shapes=[pltpu.SemaphoreType.DMA((chips,))],
        compiler_params=params(8),
    )(kept, received)
    cores = [[2 * chip + one for chip in range(chips)] for one in range(2)]
    tiles = lax.all_to_all(copies, "row", 0, 0, axis_index_groups=cores, tiled=True)
    square_out = unpack(square.reshape(pairs.shape))[None]
    tiles, square_out = barrier((tiles, square_out))
    kept, received = product(False, [jnp.concatenate(codes)], [tiles])
    second = unpack((kept + received).reshape(pairs.shape))
    sign_next = (1.5 * matrix.astype(F32) - 0.5 * scale * second).astype(BF16)
    return (square_out, sign_next[None])


def solution(mesh):
    in_specs = (P("row", "col", None), P("row", "col"), P(), P("row", "col", None), P("row", "col"))
    out_specs = (P("row", "col", None), P("row", "col", None))
    return jax.shard_map(local, mesh=mesh, in_specs=in_specs, out_specs=out_specs, check_vma=False)
```

time: 151 us -> 142 us (0.940)
  waiting for transfers between devices: 52.4 us -> 33.7 us
  starting transfers between devices: 68.8 us -> 83.1 us
  local copies, waits for them, and re-layouts: 6.85 us -> 2.98 us
  Pallas kernels: 17.6 us -> 14.9 us
    ppermute x4 -> x8, starting transfers between devices: 22.2 us -> 52.3 us  [permute(): return lax.ppermute(x, 'row', [(i, i ^ mask) for i in range(row_count)])]
    all_to_all x3 -> x2, starting transfers between devices: 36.8 us -> 15.5 us  [the longest x1 11.3 us: local(): lax.all_to_all(copies, 'row', 0, 0, axis_index_groups=cores, tiled=True)]
    all_to_all x3 -> x2, waiting for transfers between devices: 33.4 us -> 21.4 us  [the longest x1 21.4 us: local(): lax.all_to_all(copies, 'row', 0, 0, axis_index_groups=cores, tiled=True)]
    all_to_all x1, waiting for transfers between devices: 11.3 us -> 1.44 us  [local(): received = lax.all_to_all(payload, 'col', 0, 0, tiled=True)]
    ppermute x0 -> x1, starting transfers between devices: none -> 5.47 us  [local(): lax.ppermute(rows, ('row', 'col'), moves)]
    broadcast_in_dim x3 -> x0, local copies, waits for them, and re-layouts: 3.02 us -> none  [the longest x1 1.21 us: local(): jnp.broadcast_to(rows[None], (col_count,) + rows.shape)]
    pallas_call x5, Pallas kernels: 15.9 us -> 13.1 us  [the longest x2 8.28 us: product(): pl.pallas_call(lambda *refs: product_kernel(doubled, count, *refs), out_s...]
    another operation x3 -> x2, local copies, waits for them, and re-layouts: 2.84 us -> 0.82 us  [the longest x1 0.73 us: local(): square_out = unpack(square.reshape(pairs.shape))[None]]
  transfers between devices with their start and end apart: 8 -> 12, of which waited for: 5 -> 9; matrix products, arithmetic and copies ran while one was open for 2% -> 2% of each run, Pallas kernels for 6% -> 2%
where the time goes in v3:
time: 142 us; the launch traced here: 141 us
  starting transfers between devices  83.1 us (59%)
  waiting for transfers between devices  33.7 us (24%)
  Pallas kernels  14.9 us (10%)
  other arithmetic  4.48 us (3%)
  local copies, waits for them, and re-layouts  2.98 us (2%)
    ppermute x8, starting transfers between devices, permute(): return lax.ppermute(x, 'row', [(i, i ^ mask) for i in range(row_count)])  52.3 us
    all_to_all x1, waiting for transfers between devices, local(): lax.all_to_all(copies, 'row', 0, 0, axis_index_groups=cores, tiled=True)  21.4 us
    all_to_all x1, starting transfers between devices, local(): lax.all_to_all(copies, 'row', 0, 0, axis_index_groups=cores, tiled=True)  11.3 us
    all_to_all x1, starting transfers between devices, local(): received = lax.all_to_all(payload, 'col', 0, 0, tiled=True)  9.84 us
    ppermute x8, waiting for transfers between devices, permute(): return lax.ppermute(x, 'row', [(i, i ^ mask) for i in range(row_count)])  8.94 us
    pallas_call x2, Pallas kernels, product(): pl.pallas_call(lambda *refs: product_kernel(doubled, count, *refs), out_s...  8.28 us
    ppermute x1, starting transfers between devices, local(): lax.ppermute(rows, ('row', 'col'), moves)  5.47 us
    all_to_all x1, starting transfers between devices, local(): lax.all_to_all(spread(moved, col_count), 'col', 0, 0, tiled=True)  4.15 us
  transfers between devices with their start and end apart: 12, of which 9 were waited for; matrix products, arithmetic and copies ran while one was open for 2% of the time, Pallas kernels for 2%

profile of v3, /device:TPU:33, one launch (start us, length us, event | category | flops | bytes accessed | tf_op | source)
XLA Modules:
  0.0 141.0 jit_solution(1462853185610507152)
XLA Ops:
  0.6 0.8 pad_add_fusion.refs_0_
  1.4 0.0 copy-start
  1.4 1.0 copy-done
  2.4 1.7 %shard_map.68 = bf16[32,2,4224]{2,1,0:T(2,128)(2,1)} custom-call(s32[196]{0:T(256)S(1)} %pad_add_fusion.refs_0_, bf16[64,4096]{1,0:T(8,128)(2,1)S(1)} %bitcast.24), custom_call_target="tpu_custom_call" | custom-call | tf_op jit(solution)/shard_map/pallas_call | solution.py:215
  4.2 9.8 %all-to-all-start = ((bf16[32,2,4224]{2,1,0:T(2,128)(2,1)}), bf16[32,2,4224]{2,1,0:T(2,128)(2,1)S(1)}, u32[]{:S(2)}, u32[]{:S(2)}) async-start(bf16[32,2,4224]{2,1,0:T(2,128)(2,1)} %shard_map.68), calls=%async_computation | async-start | bytes 1081344 | tf_op jit(solution)/shard_map/all_to_all | solution.py:222
  14.0 0.7 fusion.8.refs_1_
  14.7 9.0 %collective-permute-start = (s32[4]{0:T(128)S(1)}, s32[4]{0:T(128)S(1)}, u32[]{:S(2)}, u32[]{:S(2)}) collective-permute-start(s32[4]{0:T(128)S(1)} %fusion.8.refs_1_), channel_id=1, source_target_pairs={{0,32},{32,0},{64,96},{96,64},{128,160},{160,128},{192,224},{224,1... | collective-permute-start | bytes 56 | tf_op jit(solution)/shard_map/ppermute | solution.py:210
  23.8 0.7 fusion.14
  24.4 0.1 collective-permute-done.refs_2_
  24.6 1.4 %all-to-all-done = bf16[32,2,4224]{2,1,0:T(2,128)(2,1)S(1)} async-done(((bf16[32,2,4224]{2,1,0:T(2,128)(2,1)}), bf16[32,2,4224]{2,1,0:T(2,128)(2,1)S(1)}, u32[]{:S(2)}, u32[]{:S(2)}) %all-to-all-start) | async-done | bytes 540704 | tf_op jit(solution)/shard_map/all_to_all | solution.py:222
  26.0 0.2 reshape.134
  26.2 0.6 convert_reduce_fusion
  26.8 0.1 reshape.141
  26.9 1.0 fusion
  27.9 0.1 reshape.135
  28.1 0.1 copy.10
  28.1 0.1 reshape.136
  28.2 9.5 %collective-permute-start.2 = (bf16[136,128]{1,0:T(8,128)(2,1)S(1)}, bf16[136,128]{1,0:T(8,128)(2,1)S(1)}, u32[]{:S(2)}, u32[]{:S(2)}) collective-permute-start(bf16[136,128]{1,0:T(8,128)(2,1)S(1)} %get-tuple-element.53), channel_id=1, source_target_pairs={{0,64},{32,96},{64,0},{96,32},{128,192},{160,224},{192,128},{224,1... | collective-permute-start | bytes 104456 | tf_op jit(solution)/shard_map/ppermute | solution.py:210
  37.7 5.5 %collective-permute-start.1 = (bf16[128,128]{1,0:T(8,128)(2,1)S(1)}, bf16[128,128]{1,0:T(8,128)(2,1)S(1)}, u32[]{:S(2)}, u32[]{:S(2)}) collective-permute-start(bf16[128,128]{1,0:T(8,128)(2,1)S(1)} %bitcast.32), channel_id=1, source_target_pairs={{0,0},{1,32},{2,2},{3,34},{4,4},{5,36},{6,6},{7,38},{8,8},{9,40},{... | collective-permute-start | bytes 98312 | tf_op jit(solution)/shard_map/ppermute | solution.py:241
  43.2 1.9 %collective-permute-done.1.tile = bf16[128,128]{1,0:T(8,128)(2,1)S(1)} collective-permute-done((bf16[128,128]{1,0:T(8,128)(2,1)S(1)}, bf16[128,128]{1,0:T(8,128)(2,1)S(1)}, u32[]{:S(2)}, u32[]{:S(2)}) %collective-permute-start.1) | collective-permute-done | bytes 32800 | tf_op jit(solution)/shard_map/ppermute | solution.py:241
  45.1 0.0 collective-permute-done.2
  45.1 1.2 shard_map.69
  46.4 4.2 %all-to-all-start.1 = ((bf16[32,128,128]{2,1,0:T(8,128)(2,1)}), bf16[32,128,128]{2,1,0:T(8,128)(2,1)S(1)}, u32[]{:S(2)}, u32[]{:S(2)}) async-start(bf16[32,128,128]{2,1,0:T(8,128)(2,1)} %shard_map.69), calls=%async_computation.1 | async-start | bytes 2097152 | tf_op jit(solution)/shard_map/all_to_all | solution.py:243
  50.6 14.0 %collective-permute-start.3 = (bf16[2,136,128]{2,1,0:T(8,128)(2,1)S(1)}, bf16[2,136,128]{2,1,0:T(8,128)(2,1)S(1)}, u32[]{:S(2)}, u32[]{:S(2)}) collective-permute-start(bf16[2,136,128]{2,1,0:T(8,128)(2,1)S(1)} %pad_maximum_fusion.2), channel_id=1, source_target_pairs={{0,512},{32,544},{64,576},{96,608},{128,640},{160,672},{192,704},{... | collective-permute-start | bytes 208904 | tf_op jit(solution)/shard_map/ppermute | solution.py:210
  64.6 1.7 %collective-permute-done.3 = bf16[2,136,128]{2,1,0:T(8,128)(2,1)S(1)} collective-permute-done((bf16[2,136,128]{2,1,0:T(8,128)(2,1)S(1)}, bf16[2,136,128]{2,1,0:T(8,128)(2,1)S(1)}, u32[]{:S(2)}, u32[]{:S(2)}) %collective-permute-start.3) | collective-permute-done | bytes 69664 | tf_op jit(solution)/shard_map/ppermute | solution.py:210
  66.3 6.7 %collective-permute-start.4 = (bf16[4,136,128]{2,1,0:T(8,128)(2,1)S(1)}, bf16[4,136,128]{2,1,0:T(8,128)(2,1)S(1)}, u32[]{:S(2)}, u32[]{:S(2)}) collective-permute-start(bf16[4,136,128]{2,1,0:T(8,128)(2,1)S(1)} %pad_maximum_fusion.1), channel_id=1, source_target_pairs={{0,256},{32,288},{64,320},{96,352},{128,384},{160,416},{192,448},{... | collective-permute-start | bytes 417800 | tf_op jit(solution)/shard_map/ppermute | solution.py:210
  73.0 0.1 convert_reduce_fusion.1
  73.1 0.1 reshape.139.codes
  73.2 4.7 %collective-permute-done.4 = bf16[4,136,128]{2,1,0:T(8,128)(2,1)S(1)} collective-permute-done((bf16[4,136,128]{2,1,0:T(8,128)(2,1)S(1)}, bf16[4,136,128]{2,1,0:T(8,128)(2,1)S(1)}, u32[]{:S(2)}, u32[]{:S(2)}) %collective-permute-start.4) | collective-permute-done | bytes 139296 | tf_op jit(solution)/shard_map/ppermute | solution.py:210
  78.0 3.7 %collective-permute-start.5 = (bf16[8,136,128]{2,1,0:T(8,128)(2,1)S(1)}, bf16[8,136,128]{2,1,0:T(8,128)(2,1)}, u32[]{:S(2)}, u32[]{:S(2)}) collective-permute-start(bf16[8,136,128]{2,1,0:T(8,128)(2,1)S(1)} %pad_maximum_fusion.refs_7_), channel_id=1, source_target_pairs={{0,128},{32,160},{64,192},{96,224},{128,0},{160,32},{192,64},{224,... | collective-permute-start | bytes 835592 | tf_op jit(solution)/shard_map/ppermute | solution.py:210
  81.6 0.1 pad_add_fusion.1.place.refs_0_
  81.7 3.5 %collective-permute-start.6 = (s32[128]{0:T(128)S(1)}, s32[128]{0:T(128)S(1)}, u32[]{:S(2)}, u32[]{:S(2)}) collective-permute-start(s32[128]{0:T(128)S(1)} %reshape.139.codes), channel_id=1, source_target_pairs={{0,32},{32,0},{64,96},{96,64},{128,160},{160,128},{192,224},{224,1... | collective-permute-start | bytes 1544 | tf_op jit(solution)/shard_map/ppermute | solution.py:210
  85.3 0.1 reshape.142.refs_5_
  85.3 0.7 collective-permute-done.6.partner_codes
  86.0 0.0 all-to-all-done.1
  86.0 2.6 %shard_map.70 = (bf16[10,512,2048]{2,1,0:T(8,128)(2,1)}, bf16[512,2048]{1,0:T(8,128)(2,1)S(1)}) custom-call(s32[128]{0:T(128)S(1)} %reshape.139.codes, s32[128]{0:T(128)S(1)} %collective-permute-done.6.partner_codes, s32[2]{0:T(128)S(1)} %pad_add_fusion.1.place.refs_0_, bf16[32,2,64,128]{3,2,1,0:T(8,128)(2,1)S(1)} %bitcast.23), custom_call_target="tpu_custom_call" | custom-call | flops 1073741824 | bytes 6291456 | tf_op jit(solution)/shard_map/pallas_call | solution.py:257
  88.7 0.0 collective-permute-done.5.refs_8_
  88.7 0.7 convert_reduce_fusion.2
  89.4 0.1 reshape.143.refs_6_
  89.5 4.3 %shard_map.71 = (f32[128,128]{1,0:T(8,128)S(1)}, f32[128,128]{1,0:T(8,128)S(1)}) custom-call(s32[2]{0:T(128)S(1)} %pad_add_fusion.1.place.refs_0_, s32[4]{0:T(128)S(1)} %fusion.8.refs_1_, s32[4]{0:T(128)S(1)} %collective-permute-done.refs_2_, bf16[10,512,2048]{2,1,0:T(8,128)(2,1)} %get-tuple-element.41.refs_3_, ...), custom_call_target="tpu_custom_call" | custom-call | flops 1073741824 | bytes 6291456 | tf_op jit(solution)/shard_map/pallas_call | solution.py:275
  93.9 2.7 %collective-permute-start.7 = (f32[128,128]{1,0:T(8,128)S(1)}, f32[128,128]{1,0:T(8,128)S(1)}, u32[]{:S(2)}, u32[]{:S(2)}) collective-permute-start(f32[128,128]{1,0:T(8,128)S(1)} %get-tuple-element.45), channel_id=1, source_target_pairs={{0,32},{32,0},{64,96},{96,64},{128,160},{160,128},{192,224},{224,1... | collective-permute-start | bytes 196616 | tf_op jit(solution)/shard_map/ppermute | solution.py:210
  96.6 0.9 collective-permute-done.7.refs_1_
  97.5 1.0 shard_map.72
  98.4 11.3 %all-to-all-start.2 = ((bf16[16,128,128]{2,1,0:T(8,128)(2,1)}), bf16[16,128,128]{2,1,0:T(8,128)(2,1)S(1)}, u32[]{:S(2)}, u32[]{:S(2)}) async-start(bf16[16,128,128]{2,1,0:T(8,128)(2,1)} %get-tuple-element.46), calls=%async_computation.2 | async-start | bytes 1048576 | tf_op jit(solution)/shard_map/all_to_all | solution.py:304
  109.7 0.1 pad_add_fusion.2.refs_5_
  109.8 0.1 reshape_reshape.4
  109.9 0.7 broadcast_in_dim_reshape.4
  110.7 21.4 %all-to-all-done.2.refs_6_ = bf16[16,128,128]{2,1,0:T(8,128)(2,1)S(1)} async-done(((bf16[16,128,128]{2,1,0:T(8,128)(2,1)}), bf16[16,128,128]{2,1,0:T(8,128)(2,1)S(1)}, u32[]{:S(2)}, u32[]{:S(2)}) %all-to-all-start.2) | async-done | bytes 524320 | tf_op jit(solution)/shard_map/all_to_all | solution.py:304
  132.0 3.9 %shard_map.73 = (f32[128,128]{1,0:T(8,128)S(1)}, f32[128,128]{1,0:T(8,128)S(1)}) custom-call(s32[2]{0:T(128)S(1)} %pad_add_fusion.1.place.refs_0_, s32[4]{0:T(128)S(1)} %fusion.8.refs_1_, s32[4]{0:T(128)S(1)} %collective-permute-done.refs_2_, bf16[10,512,2048]{2,1,0:T(8,128)(2,1)} %get-tuple-element.41.refs_3_, ...), custom_call_target="tpu_custom_call" | custom-call | flops 1073741824 | bytes 6291456 | tf_op jit(solution)/shard_map/pallas_call | solution.py:275
  136.0 3.2 %collective-permute-start.8 = (f32[128,128]{1,0:T(8,128)S(1)}, f32[128,128]{1,0:T(8,128)S(1)}, u32[]{:S(2)}, u32[]{:S(2)}) collective-permute-start(f32[128,128]{1,0:T(8,128)S(1)} %get-tuple-element.51), channel_id=1, source_target_pairs={{0,32},{32,0},{64,96},{96,64},{128,160},{160,128},{192,224},{224,1... | collective-permute-start | bytes 196616 | tf_op jit(solution)/shard_map/ppermute | solution.py:210
  139.2 0.9 collective-permute-done.8
  140.1 0.1 mul.37
  140.3 0.1 mul.39
  140.4 0.6 fusion.4
  (8 shorter events, 0.1 us)
Async XLA Ops:
  1.4 1.0 copy-start
  4.2 21.8 %all-to-all-start = ((bf16[32,2,4224]{2,1,0:T(2,128)(2,1)}), bf16[32,2,4224]{2,1,0:T(2,128)(2,1)S(1)}, u32[]{:S(2)}, u32[]{:S(2)}) async-start(bf16[32,2,4224]{2,1,0:T(2,128)(2,1)} %shard_map.68), calls=%async_computation | async-start | bytes 1081344 | tf_op jit(solution)/shard_map/all_to_all | solution.py:222
  14.7 9.9 %collective-permute-start = (s32[4]{0:T(128)S(1)}, s32[4]{0:T(128)S(1)}, u32[]{:S(2)}, u32[]{:S(2)}) collective-permute-start(s32[4]{0:T(128)S(1)} %fusion.8.refs_1_), channel_id=1, source_target_pairs={{0,32},{32,0},{64,96},{96,64},{128,160},{160,128},{192,224},{224,1... | collective-permute-start | bytes 56 | tf_op jit(solution)/shard_map/ppermute | solution.py:210
  28.2 16.9 %collective-permute-start.2 = (bf16[136,128]{1,0:T(8,128)(2,1)S(1)}, bf16[136,128]{1,0:T(8,128)(2,1)S(1)}, u32[]{:S(2)}, u32[]{:S(2)}) collective-permute-start(bf16[136,128]{1,0:T(8,128)(2,1)S(1)} %get-tuple-element.53), channel_id=1, source_target_pairs={{0,64},{32,96},{64,0},{96,32},{128,192},{160,224},{192,128},{224,1... | collective-permute-start | bytes 104456 | tf_op jit(solution)/shard_map/ppermute | solution.py:210
  37.7 7.4 %collective-permute-start.1 = (bf16[128,128]{1,0:T(8,128)(2,1)S(1)}, bf16[128,128]{1,0:T(8,128)(2,1)S(1)}, u32[]{:S(2)}, u32[]{:S(2)}) collective-permute-start(bf16[128,128]{1,0:T(8,128)(2,1)S(1)} %bitcast.32), channel_id=1, source_target_pairs={{0,0},{1,32},{2,2},{3,34},{4,4},{5,36},{6,6},{7,38},{8,8},{9,40},{... | collective-permute-start | bytes 98312 | tf_op jit(solution)/shard_map/ppermute | solution.py:241
  46.4 39.7 %all-to-all-start.1 = ((bf16[32,128,128]{2,1,0:T(8,128)(2,1)}), bf16[32,128,128]{2,1,0:T(8,128)(2,1)S(1)}, u32[]{:S(2)}, u32[]{:S(2)}) async-start(bf16[32,128,128]{2,1,0:T(8,128)(2,1)} %shard_map.69), calls=%async_computation.1 | async-start | bytes 2097152 | tf_op jit(solution)/shard_map/all_to_all | solution.py:243
  50.6 15.7 %collective-permute-start.3 = (bf16[2,136,128]{2,1,0:T(8,128)(2,1)S(1)}, bf16[2,136,128]{2,1,0:T(8,128)(2,1)S(1)}, u32[]{:S(2)}, u32[]{:S(2)}) collective-permute-start(bf16[2,136,128]{2,1,0:T(8,128)(2,1)S(1)} %pad_maximum_fusion.2), channel_id=1, source_target_pairs={{0,512},{32,544},{64,576},{96,608},{128,640},{160,672},{192,704},{... | collective-permute-start | bytes 208904 | tf_op jit(solution)/shard_map/ppermute | solution.py:210
  66.3 11.6 %collective-permute-start.4 = (bf16[4,136,128]{2,1,0:T(8,128)(2,1)S(1)}, bf16[4,136,128]{2,1,0:T(8,128)(2,1)S(1)}, u32[]{:S(2)}, u32[]{:S(2)}) collective-permute-start(bf16[4,136,128]{2,1,0:T(8,128)(2,1)S(1)} %pad_maximum_fusion.1), channel_id=1, source_target_pairs={{0,256},{32,288},{64,320},{96,352},{128,384},{160,416},{192,448},{... | collective-permute-start | bytes 417800 | tf_op jit(solution)/shard_map/ppermute | solution.py:210
  78.0 10.7 %collective-permute-start.5 = (bf16[8,136,128]{2,1,0:T(8,128)(2,1)S(1)}, bf16[8,136,128]{2,1,0:T(8,128)(2,1)}, u32[]{:S(2)}, u32[]{:S(2)}) collective-permute-start(bf16[8,136,128]{2,1,0:T(8,128)(2,1)S(1)} %pad_maximum_fusion.refs_7_), channel_id=1, source_target_pairs={{0,128},{32,160},{64,192},{96,224},{128,0},{160,32},{192,64},{224,... | collective-permute-start | bytes 835592 | tf_op jit(solution)/shard_map/ppermute | solution.py:210
  81.7 4.3 %collective-permute-start.6 = (s32[128]{0:T(128)S(1)}, s32[128]{0:T(128)S(1)}, u32[]{:S(2)}, u32[]{:S(2)}) collective-permute-start(s32[128]{0:T(128)S(1)} %reshape.139.codes), channel_id=1, source_target_pairs={{0,32},{32,0},{64,96},{96,64},{128,160},{160,128},{192,224},{224,1... | collective-permute-start | bytes 1544 | tf_op jit(solution)/shard_map/ppermute | solution.py:210
  93.9 3.6 %collective-permute-start.7 = (f32[128,128]{1,0:T(8,128)S(1)}, f32[128,128]{1,0:T(8,128)S(1)}, u32[]{:S(2)}, u32[]{:S(2)}) collective-permute-start(f32[128,128]{1,0:T(8,128)S(1)} %get-tuple-element.45), channel_id=1, source_target_pairs={{0,32},{32,0},{64,96},{96,64},{128,160},{160,128},{192,224},{224,1... | collective-permute-start | bytes 196616 | tf_op jit(solution)/shard_map/ppermute | solution.py:210
  98.4 33.6 %all-to-all-start.2 = ((bf16[16,128,128]{2,1,0:T(8,128)(2,1)}), bf16[16,128,128]{2,1,0:T(8,128)(2,1)S(1)}, u32[]{:S(2)}, u32[]{:S(2)}) async-start(bf16[16,128,128]{2,1,0:T(8,128)(2,1)} %get-tuple-element.46), calls=%async_computation.2 | async-start | bytes 1048576 | tf_op jit(solution)/shard_map/all_to_all | solution.py:304
  136.0 4.1 %collective-permute-start.8 = (f32[128,128]{1,0:T(8,128)S(1)}, f32[128,128]{1,0:T(8,128)S(1)}, u32[]{:S(2)}, u32[]{:S(2)}) collective-permute-start(f32[128,128]{1,0:T(8,128)S(1)} %get-tuple-element.51), channel_id=1, source_target_pairs={{0,32},{32,0},{64,96},{96,64},{128,160},{160,128},{192,224},{224,1... | collective-permute-start | bytes 196616 | tf_op jit(solution)/shard_map/ppermute | solution.py:210

commit v4 on v3

--- a/solution.py
+++ b/solution.py
@@ -56,15 +56,9 @@
             dense[rows, columns] = dense[rows, columns] + block
 
 
-def payload_kernel(places_per, count, words, blocks, payload):
+def tail_kernel(places_per, count, words, tail):
     shift = count.bit_length() - 1
-    width = blocks.shape[-1]
-    items = payload.shape[0] * places_per
-    for first in range(0, blocks.shape[0], 16):
-        owners = pl.ds(first // places_per, 16 // places_per)
-        payload[owners, :, :width] = blocks[first : first + 16].reshape(
-            16 // places_per, places_per, width
-        )
+    items = tail.shape[0] * places_per
     lane = lax.broadcasted_iota(I32, (1, LANES), 1)
     base = jnp.zeros((1, LANES), I32)
     for slot in range(SLOTS):
@@ -81,10 +75,44 @@
             block_column = words[items + (safe & (count - 1))] & (SIDE - 1)
             spot = jnp.where(task < 0, -1, block_row * SIDE + block_column)
             rows.append(jnp.where(lane == 0, spot, base))
-        payload[j, :, width:] = jnp.concatenate(rows, axis=0).astype(F32).astype(BF16)
+        tail[j] = jnp.concatenate(rows, axis=0).astype(F32).astype(BF16)
         return carry
 
-    lax.fori_loop(0, payload.shape[0], body, 0, unroll=8)
+    lax.fori_loop(0, tail.shape[0], body, 0, unroll=8)
+
+
+def payload_kernel(places_per, tail, blocks, payload):
+    width = blocks.shape[-1]
+    for first in range(0, blocks.shape[0], 16):
+        owners = pl.ds(first // places_per, 16 // places_per)
+        payload[owners, :, :width] = blocks[first : first + 16].reshape(
+            16 // places_per, places_per, width
+        )
+    payload[:, :, width:] = tail[...]
+
+
+def combine_kernel(own, received, before, matrix):
+    width = before.shape[-1]
+    per, cap = 16 // received.shape[1], received.shape[1]
+    lane = lax.broadcasted_iota(I32, (1, 8), 1)
+    spots = jnp.full((1, 8), -2, I32)
+    for slot in range(SLOTS):
+        spots = jnp.where(lane == slot, own[slot], spots)
+    spots = spots.astype(F32)
+    total = jnp.zeros((8, width), F32)
+    parts, marks = [], []
+    for first in range(0, received.shape[0], per):
+        part = received[first : first + per].reshape(per * cap, received.shape[2])
+        parts.append(part[:, :width])
+        place = part[:, width : width + LANES].astype(F32)[:, :1]
+        marks.append(jnp.where(place == spots, 1.0, 0.0).astype(BF16))
+    total = lax.dot_general(
+        jnp.concatenate(marks, axis=0),
+        jnp.concatenate(parts, axis=0),
+        (((0,), (0,)), ((), ())),
+        preferred_element_type=F32,
+    )
+    matrix[...] = (before[...].astype(F32) + total[:SLOTS]).astype(BF16)
 
 
 def spread_kernel(tile, copies, sems):
@@ -212,21 +240,32 @@
     cap = grid_tasks.shape[1] // col_count
     width = grid_blocks.shape[-1]
     words = jnp.concatenate([grid_tasks[0], block_perm, own_codes])
+    tail = pl.pallas_call(
+        lambda *refs: tail_kernel(cap, block_count, *refs),
+        out_shape=jax.ShapeDtypeStruct((col_count, cap, LANES), BF16),
+        in_specs=[SMEM],
+        out_specs=VMEM,
+        compiler_params=params(8),
+    )(words)
     payload = pl.pallas_call(
-        lambda *refs: payload_kernel(cap, block_count, *refs),
+        lambda *refs: payload_kernel(cap, *refs),
         out_shape=jax.ShapeDtypeStruct((col_count, cap, width + LANES), BF16),
-        in_specs=[SMEM, VMEM],
+        in_specs=[VMEM] * 2,
         out_specs=VMEM,
         compiler_params=params(8),
-    )(words, grid_blocks[0])
+    )(tail, grid_blocks[0])
     received = lax.all_to_all(payload, "col", 0, 0, tiled=True)
-    received, theirs = barrier((received, permute(own_place, 1)))
+    received, theirs, stored = barrier(
+        (received, permute(own_place, 1), matrix_blocks[0].astype(F32))
+    )
     codes_left = received[:, 0, width + 1 : width + 1 + SLOTS].astype(I32).reshape(-1)
-    arrived_place = received[:, :, width].astype(I32).reshape(-1)
-    items = received.reshape(-1, width + LANES)
-    matches = (own_place[:, None] == arrived_place[None, :]).astype(BF16)
-    grid_sum = jnp.dot(matches, items, preferred_element_type=F32)[:, :width]
-    matrix = (matrix_blocks[0].astype(F32) + grid_sum).astype(BF16)
+    matrix = pl.pallas_call(
+        combine_kernel,
+        out_shape=jax.ShapeDtypeStruct((SLOTS, width), BF16),
+        in_specs=[SMEM] + [VMEM] * 2,
+        out_specs=VMEM,
+        compiler_params=params(8),
+    )(own_place, received, stored)
     pairs = barrier(pack(matrix))
 
     moves = []

time: 142 us -> 144 us (1.014)
  waiting for transfers between devices: 33.7 us -> 49.5 us
  starting transfers between devices: 83.1 us -> 69.8 us
    ppermute x8, starting transfers between devices: 52.3 us -> 33.8 us  [permute(): return lax.ppermute(x, 'row', [(i, i ^ mask) for i in range(row_count)])]
    all_to_all x1, waiting for transfers between devices: 1.44 us -> 16.3 us  [local(): received = lax.all_to_all(payload, 'col', 0, 0, tiled=True)]
    all_to_all x1, starting transfers between devices: 9.84 us -> 16 us  [local(): received = lax.all_to_all(payload, 'col', 0, 0, tiled=True)]
    ppermute x1, starting transfers between devices: 5.47 us -> 3.71 us  [local(): lax.ppermute(rows, ('row', 'col'), moves)]
  transfers between devices with their start and end apart: 12 -> 12, of which waited for: 9 -> 9; matrix products, arithmetic and copies ran while one was open for 2% -> 2% of each run, Pallas kernels for 2% -> 3%
where the time goes in v4:
time: 144 us; the launch traced here: 143 us
  starting transfers between devices  69.8 us (48%)
  waiting for transfers between devices  49.5 us (34%)
  Pallas kernels  15.7 us (11%)
  other arithmetic  4.63 us (3%)
  local copies, waits for them, and re-layouts  2.66 us (2%)
    ppermute x8, starting transfers between devices, permute(): return lax.ppermute(x, 'row', [(i, i ^ mask) for i in range(row_count)])  33.8 us
    all_to_all x1, waiting for transfers between devices, local(): lax.all_to_all(copies, 'row', 0, 0, axis_index_groups=cores, tiled=True)  21.4 us
    all_to_all x1, waiting for transfers between devices, local(): received = lax.all_to_all(payload, 'col', 0, 0, tiled=True)  16.3 us
    all_to_all x1, starting transfers between devices, local(): received = lax.all_to_all(payload, 'col', 0, 0, tiled=True)  16 us
    all_to_all x1, starting transfers between devices, local(): lax.all_to_all(copies, 'row', 0, 0, axis_index_groups=cores, tiled=True)  11.2 us
    ppermute x8, waiting for transfers between devices, permute(): return lax.ppermute(x, 'row', [(i, i ^ mask) for i in range(row_count)])  10.1 us
    pallas_call x2, Pallas kernels, product(): pl.pallas_call(lambda *refs: product_kernel(doubled, count, *refs), out_s...  8.28 us
    all_to_all x1, starting transfers between devices, local(): lax.all_to_all(spread(moved, col_count), 'col', 0, 0, tiled=True)  5.1 us
  transfers between devices with their start and end apart: 12, of which 9 were waited for; matrix products, arithmetic and copies ran while one was open for 2% of the time, Pallas kernels for 3%

profile of v4, /device:TPU:33, one launch (start us, length us, event | category | flops | bytes accessed | tf_op | source)
XLA Modules:
  0.0 143.2 jit_solution(14666699366199736974)
XLA Ops:
  0.6 0.7 fusion.3.own.refs_1_
  1.3 2.6 %collective-permute-start = (s32[4]{0:T(128)S(1)}, s32[4]{0:T(128)S(1)}, u32[]{:S(2)}, u32[]{:S(2)}) collective-permute-start(s32[4]{0:T(128)S(1)} %fusion.3.own.refs_1_), channel_id=1, source_target_pairs={{0,32},{32,0},{64,96},{96,64},{128,160},{160,128},{192,224},{224,1... | collective-permute-start | bytes 56 | tf_op jit(solution)/shard_map/ppermute | solution.py:238
  3.9 0.8 pad_add_fusion.refs_0_
  4.7 0.9 shard_map.68.refs_0_
  5.6 0.0 copy-start
  5.6 1.0 copy-done
  6.6 0.9 shard_map.69
  7.5 16.0 %all-to-all-start = ((bf16[32,2,4224]{2,1,0:T(2,128)(2,1)}), bf16[32,2,4224]{2,1,0:T(2,128)(2,1)S(1)}, u32[]{:S(2)}, u32[]{:S(2)}) async-start(bf16[32,2,4224]{2,1,0:T(2,128)(2,1)} %shard_map.69), calls=%async_computation | async-start | bytes 1081344 | tf_op jit(solution)/shard_map/all_to_all | solution.py:257
  23.5 0.7 fusion.9
  24.2 0.8 bitcast_convert_fusion.before
  25.0 0.0 collective-permute-done.refs_2_
  25.0 16.3 %all-to-all-done.received = bf16[32,2,4224]{2,1,0:T(2,128)(2,1)S(1)} async-done(((bf16[32,2,4224]{2,1,0:T(2,128)(2,1)}), bf16[32,2,4224]{2,1,0:T(2,128)(2,1)S(1)}, u32[]{:S(2)}, u32[]{:S(2)}) %all-to-all-start) | async-done | bytes 540704 | tf_op jit(solution)/shard_map/all_to_all | solution.py:257
  41.3 0.9 shard_map.70
  42.2 0.1 reshape.63
  42.3 0.1 copy.10
  42.4 0.1 reshape.64
  42.5 1.9 %collective-permute-start.2 = (bf16[136,128]{1,0:T(8,128)(2,1)S(1)}, bf16[136,128]{1,0:T(8,128)(2,1)S(1)}, u32[]{:S(2)}, u32[]{:S(2)}) collective-permute-start(bf16[136,128]{1,0:T(8,128)(2,1)S(1)} %get-tuple-element.55), channel_id=1, source_target_pairs={{0,64},{32,96},{64,0},{96,32},{128,192},{160,224},{192,128},{224,1... | collective-permute-start | bytes 104456 | tf_op jit(solution)/shard_map/ppermute | solution.py:238
  44.4 3.7 %collective-permute-start.1 = (bf16[128,128]{1,0:T(8,128)(2,1)S(1)}, bf16[128,128]{1,0:T(8,128)(2,1)S(1)}, u32[]{:S(2)}, u32[]{:S(2)}) collective-permute-start(bf16[128,128]{1,0:T(8,128)(2,1)S(1)} %bitcast.32), channel_id=1, source_target_pairs={{0,0},{1,32},{2,2},{3,34},{4,4},{5,36},{6,6},{7,38},{8,8},{9,40},{... | collective-permute-start | bytes 98312 | tf_op jit(solution)/shard_map/ppermute | solution.py:280
  48.1 1.7 %collective-permute-done.1.tile = bf16[128,128]{1,0:T(8,128)(2,1)S(1)} collective-permute-done((bf16[128,128]{1,0:T(8,128)(2,1)S(1)}, bf16[128,128]{1,0:T(8,128)(2,1)S(1)}, u32[]{:S(2)}, u32[]{:S(2)}) %collective-permute-start.1) | collective-permute-done | bytes 32800 | tf_op jit(solution)/shard_map/ppermute | solution.py:280
  49.8 1.3 collective-permute-done.2
  51.1 1.3 shard_map.71
  52.3 5.1 %all-to-all-start.1 = ((bf16[32,128,128]{2,1,0:T(8,128)(2,1)}), bf16[32,128,128]{2,1,0:T(8,128)(2,1)S(1)}, u32[]{:S(2)}, u32[]{:S(2)}) async-start(bf16[32,128,128]{2,1,0:T(8,128)(2,1)} %shard_map.71), calls=%async_computation.1 | async-start | bytes 2097152 | tf_op jit(solution)/shard_map/all_to_all | solution.py:282
  57.5 9.5 %collective-permute-start.3 = (bf16[2,136,128]{2,1,0:T(8,128)(2,1)S(1)}, bf16[2,136,128]{2,1,0:T(8,128)(2,1)S(1)}, u32[]{:S(2)}, u32[]{:S(2)}) collective-permute-start(bf16[2,136,128]{2,1,0:T(8,128)(2,1)S(1)} %pad_maximum_fusion.2), channel_id=1, source_target_pairs={{0,512},{32,544},{64,576},{96,608},{128,640},{160,672},{192,704},{... | collective-permute-start | bytes 208904 | tf_op jit(solution)/shard_map/ppermute | solution.py:238
  67.0 2.0 %collective-permute-done.3 = bf16[2,136,128]{2,1,0:T(8,128)(2,1)S(1)} collective-permute-done((bf16[2,136,128]{2,1,0:T(8,128)(2,1)S(1)}, bf16[2,136,128]{2,1,0:T(8,128)(2,1)S(1)}, u32[]{:S(2)}, u32[]{:S(2)}) %collective-permute-start.3) | collective-permute-done | bytes 69664 | tf_op jit(solution)/shard_map/ppermute | solution.py:238
  69.0 6.4 %collective-permute-start.4 = (bf16[4,136,128]{2,1,0:T(8,128)(2,1)S(1)}, bf16[4,136,128]{2,1,0:T(8,128)(2,1)S(1)}, u32[]{:S(2)}, u32[]{:S(2)}) collective-permute-start(bf16[4,136,128]{2,1,0:T(8,128)(2,1)S(1)} %pad_maximum_fusion.1), channel_id=1, source_target_pairs={{0,256},{32,288},{64,320},{96,352},{128,384},{160,416},{192,448},{... | collective-permute-start | bytes 417800 | tf_op jit(solution)/shard_map/ppermute | solution.py:238
  75.4 0.1 convert_reduce_fusion
  75.5 0.1 reshape.68.codes
  75.6 4.4 %collective-permute-done.4 = bf16[4,136,128]{2,1,0:T(8,128)(2,1)S(1)} collective-permute-done((bf16[4,136,128]{2,1,0:T(8,128)(2,1)S(1)}, bf16[4,136,128]{2,1,0:T(8,128)(2,1)S(1)}, u32[]{:S(2)}, u32[]{:S(2)}) %collective-permute-start.4) | collective-permute-done | bytes 139296 | tf_op jit(solution)/shard_map/ppermute | solution.py:238
  80.0 4.1 %collective-permute-start.5 = (bf16[8,136,128]{2,1,0:T(8,128)(2,1)S(1)}, bf16[8,136,128]{2,1,0:T(8,128)(2,1)}, u32[]{:S(2)}, u32[]{:S(2)}) collective-permute-start(bf16[8,136,128]{2,1,0:T(8,128)(2,1)S(1)} %pad_maximum_fusion.refs_7_), channel_id=1, source_target_pairs={{0,128},{32,160},{64,192},{96,224},{128,0},{160,32},{192,64},{224,... | collective-permute-start | bytes 835592 | tf_op jit(solution)/shard_map/ppermute | solution.py:238
  84.1 0.1 pad_add_fusion.1.place.refs_0_
  84.2 3.4 %collective-permute-start.6 = (s32[128]{0:T(128)S(1)}, s32[128]{0:T(128)S(1)}, u32[]{:S(2)}, u32[]{:S(2)}) collective-permute-start(s32[128]{0:T(128)S(1)} %reshape.68.codes), channel_id=1, source_target_pairs={{0,32},{32,0},{64,96},{96,64},{128,160},{160,128},{192,224},{224,1... | collective-permute-start | bytes 1544 | tf_op jit(solution)/shard_map/ppermute | solution.py:238
  87.6 0.1 reshape.69.refs_5_
  87.7 0.7 collective-permute-done.6.partner_codes
  88.4 0.0 all-to-all-done.1
  88.4 2.6 %shard_map.72 = (bf16[10,512,2048]{2,1,0:T(8,128)(2,1)}, bf16[512,2048]{1,0:T(8,128)(2,1)S(1)}) custom-call(s32[128]{0:T(128)S(1)} %reshape.68.codes, s32[128]{0:T(128)S(1)} %collective-permute-done.6.partner_codes, s32[2]{0:T(128)S(1)} %pad_add_fusion.1.place.refs_0_, bf16[32,2,64,128]{3,2,1,0:T(8,128)(2,1)S(1)} %bitcast.23), custom_call_target="tpu_custom_call" | custom-call | flops 1073741824 | bytes 6291456 | tf_op jit(solution)/shard_map/pallas_call | solution.py:296
  91.0 0.0 collective-permute-done.5.refs_8_
  91.0 0.7 convert_reduce_fusion.1
  91.8 0.1 reshape.70.refs_6_
  91.9 4.3 %shard_map.73 = (f32[128,128]{1,0:T(8,128)S(1)}, f32[128,128]{1,0:T(8,128)S(1)}) custom-call(s32[2]{0:T(128)S(1)} %pad_add_fusion.1.place.refs_0_, s32[4]{0:T(128)S(1)} %fusion.3.own.refs_1_, s32[4]{0:T(128)S(1)} %collective-permute-done.refs_2_, bf16[10,512,2048]{2,1,0:T(8,128)(2,1)} %get-tuple-element.43.refs_3_, ...), custom_call_target="tpu_custom_call" | custom-call | flops 1073741824 | bytes 6291456 | tf_op jit(solution)/shard_map/pallas_call | solution.py:314
  96.2 2.7 %collective-permute-start.7 = (f32[128,128]{1,0:T(8,128)S(1)}, f32[128,128]{1,0:T(8,128)S(1)}, u32[]{:S(2)}, u32[]{:S(2)}) collective-permute-start(f32[128,128]{1,0:T(8,128)S(1)} %get-tuple-element.47), channel_id=1, source_target_pairs={{0,32},{32,0},{64,96},{96,64},{128,160},{160,128},{192,224},{224,1... | collective-permute-start | bytes 196616 | tf_op jit(solution)/shard_map/ppermute | solution.py:238
  98.9 0.9 collective-permute-done.7.refs_1_
  99.8 1.0 shard_map.74
  100.8 11.2 %all-to-all-start.2 = ((bf16[16,128,128]{2,1,0:T(8,128)(2,1)}), bf16[16,128,128]{2,1,0:T(8,128)(2,1)S(1)}, u32[]{:S(2)}, u32[]{:S(2)}) async-start(bf16[16,128,128]{2,1,0:T(8,128)(2,1)} %get-tuple-element.48), calls=%async_computation.2 | async-start | bytes 1048576 | tf_op jit(solution)/shard_map/all_to_all | solution.py:343
  112.0 0.1 pad_add_fusion.2.refs_5_
  112.0 0.1 reshape_reshape.4
  112.1 0.7 broadcast_in_dim_reshape.3
  112.9 21.4 %all-to-all-done.2.refs_6_ = bf16[16,128,128]{2,1,0:T(8,128)(2,1)S(1)} async-done(((bf16[16,128,128]{2,1,0:T(8,128)(2,1)}), bf16[16,128,128]{2,1,0:T(8,128)(2,1)S(1)}, u32[]{:S(2)}, u32[]{:S(2)}) %all-to-all-start.2) | async-done | bytes 524320 | tf_op jit(solution)/shard_map/all_to_all | solution.py:343
  134.2 3.9 %shard_map.75 = (f32[128,128]{1,0:T(8,128)S(1)}, f32[128,128]{1,0:T(8,128)S(1)}) custom-call(s32[2]{0:T(128)S(1)} %pad_add_fusion.1.place.refs_0_, s32[4]{0:T(128)S(1)} %fusion.3.own.refs_1_, s32[4]{0:T(128)S(1)} %collective-permute-done.refs_2_, bf16[10,512,2048]{2,1,0:T(8,128)(2,1)} %get-tuple-element.43.refs_3_, ...), custom_call_target="tpu_custom_call" | custom-call | flops 1073741824 | bytes 6291456 | tf_op jit(solution)/shard_map/pallas_call | solution.py:314
  138.2 3.2 %collective-permute-start.8 = (f32[128,128]{1,0:T(8,128)S(1)}, f32[128,128]{1,0:T(8,128)S(1)}, u32[]{:S(2)}, u32[]{:S(2)}) collective-permute-start(f32[128,128]{1,0:T(8,128)S(1)} %get-tuple-element.53), channel_id=1, source_target_pairs={{0,32},{32,0},{64,96},{96,64},{128,160},{160,128},{192,224},{224,1... | collective-permute-start | bytes 196616 | tf_op jit(solution)/shard_map/ppermute | solution.py:238
  141.4 0.9 collective-permute-done.8
  142.3 0.1 mul.33
  142.5 0.1 mul.35
  142.6 0.6 fusion.2
  (8 shorter events, 0.1 us)
Async XLA Ops:
  1.3 23.7 %collective-permute-start = (s32[4]{0:T(128)S(1)}, s32[4]{0:T(128)S(1)}, u32[]{:S(2)}, u32[]{:S(2)}) collective-permute-start(s32[4]{0:T(128)S(1)} %fusion.3.own.refs_1_), channel_id=1, source_target_pairs={{0,32},{32,0},{64,96},{96,64},{128,160},{160,128},{192,224},{224,1... | collective-permute-start | bytes 56 | tf_op jit(solution)/shard_map/ppermute | solution.py:238
  5.6 1.0 copy-start
  7.5 33.8 %all-to-all-start = ((bf16[32,2,4224]{2,1,0:T(2,128)(2,1)}), bf16[32,2,4224]{2,1,0:T(2,128)(2,1)S(1)}, u32[]{:S(2)}, u32[]{:S(2)}) async-start(bf16[32,2,4224]{2,1,0:T(2,128)(2,1)} %shard_map.69), calls=%async_computation | async-start | bytes 1081344 | tf_op jit(solution)/shard_map/all_to_all | solution.py:257
  42.5 8.6 %collective-permute-start.2 = (bf16[136,128]{1,0:T(8,128)(2,1)S(1)}, bf16[136,128]{1,0:T(8,128)(2,1)S(1)}, u32[]{:S(2)}, u32[]{:S(2)}) collective-permute-start(bf16[136,128]{1,0:T(8,128)(2,1)S(1)} %get-tuple-element.55), channel_id=1, source_target_pairs={{0,64},{32,96},{64,0},{96,32},{128,192},{160,224},{192,128},{224,1... | collective-permute-start | bytes 104456 | tf_op jit(solution)/shard_map/ppermute | solution.py:238
  44.4 5.4 %collective-permute-start.1 = (bf16[128,128]{1,0:T(8,128)(2,1)S(1)}, bf16[128,128]{1,0:T(8,128)(2,1)S(1)}, u32[]{:S(2)}, u32[]{:S(2)}) collective-permute-start(bf16[128,128]{1,0:T(8,128)(2,1)S(1)} %bitcast.32), channel_id=1, source_target_pairs={{0,0},{1,32},{2,2},{3,34},{4,4},{5,36},{6,6},{7,38},{8,8},{9,40},{... | collective-permute-start | bytes 98312 | tf_op jit(solution)/shard_map/ppermute | solution.py:280
  52.3 36.1 %all-to-all-start.1 = ((bf16[32,128,128]{2,1,0:T(8,128)(2,1)}), bf16[32,128,128]{2,1,0:T(8,128)(2,1)S(1)}, u32[]{:S(2)}, u32[]{:S(2)}) async-start(bf16[32,128,128]{2,1,0:T(8,128)(2,1)} %shard_map.71), calls=%async_computation.1 | async-start | bytes 2097152 | tf_op jit(solution)/shard_map/all_to_all | solution.py:282
  57.5 11.5 %collective-permute-start.3 = (bf16[2,136,128]{2,1,0:T(8,128)(2,1)S(1)}, bf16[2,136,128]{2,1,0:T(8,128)(2,1)S(1)}, u32[]{:S(2)}, u32[]{:S(2)}) collective-permute-start(bf16[2,136,128]{2,1,0:T(8,128)(2,1)S(1)} %pad_maximum_fusion.2), channel_id=1, source_target_pairs={{0,512},{32,544},{64,576},{96,608},{128,640},{160,672},{192,704},{... | collective-permute-start | bytes 208904 | tf_op jit(solution)/shard_map/ppermute | solution.py:238
  69.0 11.0 %collective-permute-start.4 = (bf16[4,136,128]{2,1,0:T(8,128)(2,1)S(1)}, bf16[4,136,128]{2,1,0:T(8,128)(2,1)S(1)}, u32[]{:S(2)}, u32[]{:S(2)}) collective-permute-start(bf16[4,136,128]{2,1,0:T(8,128)(2,1)S(1)} %pad_maximum_fusion.1), channel_id=1, source_target_pairs={{0,256},{32,288},{64,320},{96,352},{128,384},{160,416},{192,448},{... | collective-permute-start | bytes 417800 | tf_op jit(solution)/shard_map/ppermute | solution.py:238
  80.0 11.0 %collective-permute-start.5 = (bf16[8,136,128]{2,1,0:T(8,128)(2,1)S(1)}, bf16[8,136,128]{2,1,0:T(8,128)(2,1)}, u32[]{:S(2)}, u32[]{:S(2)}) collective-permute-start(bf16[8,136,128]{2,1,0:T(8,128)(2,1)S(1)} %pad_maximum_fusion.refs_7_), channel_id=1, source_target_pairs={{0,128},{32,160},{64,192},{96,224},{128,0},{160,32},{192,64},{224,... | collective-permute-start | bytes 835592 | tf_op jit(solution)/shard_map/ppermute | solution.py:238
  84.2 4.2 %collective-permute-start.6 = (s32[128]{0:T(128)S(1)}, s32[128]{0:T(128)S(1)}, u32[]{:S(2)}, u32[]{:S(2)}) collective-permute-start(s32[128]{0:T(128)S(1)} %reshape.68.codes), channel_id=1, source_target_pairs={{0,32},{32,0},{64,96},{96,64},{128,160},{160,128},{192,224},{224,1... | collective-permute-start | bytes 1544 | tf_op jit(solution)/shard_map/ppermute | solution.py:238
  96.2 3.6 %collective-permute-start.7 = (f32[128,128]{1,0:T(8,128)S(1)}, f32[128,128]{1,0:T(8,128)S(1)}, u32[]{:S(2)}, u32[]{:S(2)}) collective-permute-start(f32[128,128]{1,0:T(8,128)S(1)} %get-tuple-element.47), channel_id=1, source_target_pairs={{0,32},{32,0},{64,96},{96,64},{128,160},{160,128},{192,224},{224,1... | collective-permute-start | bytes 196616 | tf_op jit(solution)/shard_map/ppermute | solution.py:238
  100.8 33.5 %all-to-all-start.2 = ((bf16[16,128,128]{2,1,0:T(8,128)(2,1)}), bf16[16,128,128]{2,1,0:T(8,128)(2,1)S(1)}, u32[]{:S(2)}, u32[]{:S(2)}) async-start(bf16[16,128,128]{2,1,0:T(8,128)(2,1)} %get-tuple-element.48), calls=%async_computation.2 | async-start | bytes 1048576 | tf_op jit(solution)/shard_map/all_to_all | solution.py:343
  138.2 4.1 %collective-permute-start.8 = (f32[128,128]{1,0:T(8,128)S(1)}, f32[128,128]{1,0:T(8,128)S(1)}, u32[]{:S(2)}, u32[]{:S(2)}) collective-permute-start(f32[128,128]{1,0:T(8,128)S(1)} %get-tuple-element.53), channel_id=1, source_target_pairs={{0,32},{32,0},{64,96},{96,64},{128,160},{160,128},{192,224},{224,1... | collective-permute-start | bytes 196616 | tf_op jit(solution)/shard_map/ppermute | solution.py:238
